TPU v7x, 32 devices: a whole 2x2x4 slice. The times are simulated.
32 devices in a mesh: wide: 8 (over z, core), narrow: 4 (over y, x).
Axes of the slice: x: 2, y: 2, z: 4, core: 2. Of those that a mesh axis runs over, the one named last changes fastest.
Arguments:
- source: float32 [128, 512, 128], P('wide', 'narrow'), may hold values from -14 to 14, as said below
- reaction: float32 [128, 512, 128], P('wide', 'narrow'), may hold values from 0.02 to 0.2
- conductance: float32 [128, 512, 128], P('wide', 'narrow'), may hold values from 0.25 to 2
- coarse_inverse: float32 [8, 4, 8, 256], P('wide', 'narrow'), may hold values from -1 to 16, as said below
Outputs:
- solution: float32 [128, 512, 128], P('wide', 'narrow')
- residual: float32 [128, 512, 128], P('wide', 'narrow')
- direction: float32 [128, 512, 128], P('wide', 'narrow')
Inputs may be any that keep to these rules, and one draw needn't show every extreme that they name: source: finite values of either sign. coarse_inverse: a symmetric positive definite matrix.
All inputs are finite; a program needn't handle non-finite values.
Results may differ from a plain program's by a relative error of at most 0.0003.
Values sent between devices are 32-bit elements; how exact they have to be, the bound alone decides.
A program may use at most 64 MiB of HBM per device.

v0:
```python
import jax
import jax.numpy as jnp
from jax import lax
from jax.sharding import PartitionSpec as P

W = 8
PRIMAL = 8
ITERS = 2


SHIFT = 0.06
KAPPA = 1.0


def with_halo(block, sides, width):
    for axis, dim in sides:
        count = lax.axis_size(axis)
        forward = [(i, i + 1) for i in range(count - 1)]
        backward = [(target, source) for source, target in forward]
        low = lax.ppermute(
            lax.slice_in_dim(block, block.shape[dim] - width, None, axis=dim), axis, forward
        )
        high = lax.ppermute(lax.slice_in_dim(block, 0, width, axis=dim), axis, backward)
        block = jnp.concatenate([low, block, high], axis=dim)
    return block


def passed_along(block, axis, distance):
    devices = range(lax.axis_size(axis))
    route = [(i - distance, i) for i in devices if i - distance in devices]
    return lax.ppermute(block, axis, route)


def sine_basis(extent):
    indices = jnp.arange(extent, dtype=jnp.float32) + 1.0
    angles = jnp.pi * indices[:, None] * indices[None, :] / (extent + 1)
    sine_table = jnp.sqrt(2.0 / (extent + 1)) * jnp.sin(angles)
    eigenvalues = 2.0 - 2.0 * jnp.cos(jnp.pi * indices / (extent + 1))
    return (sine_table, eigenvalues)


def harmonic(first, second):
    return 2.0 * first * second / (first + second)


def face_weights(padded_cond, conductance):
    face_x = harmonic(padded_cond[:-1, 1:-1], padded_cond[1:, 1:-1])
    face_y = harmonic(padded_cond[1:-1, :-1], padded_cond[1:-1, 1:])
    face_z = harmonic(conductance[:, :, :-1], conductance[:, :, 1:])
    return (face_x, face_y, face_z)


def operate(field, padded_field, reaction, face_x, face_y, face_z):
    result = reaction * field
    result = (
        result
        + face_x[1:] * (field - padded_field[2:, 1:-1])
        + face_x[:-1] * (field - padded_field[:-2, 1:-1])
    )
    result = (
        result
        + face_y[:, 1:] * (field - padded_field[1:-1, 2:])
        + face_y[:, :-1] * (field - padded_field[1:-1, :-2])
    )
    flux_z = face_z * (field[:, :, :-1] - field[:, :, 1:])
    return (
        result
        + jnp.pad(flux_z, ((0, 0), (0, 0), (0, 1)))
        - jnp.pad(flux_z, ((0, 0), (0, 0), (1, 0)))
    )


def transform_first(field, table_x):
    return jnp.einsum("ryz,re->eyz", field, table_x, precision=lax.Precision.HIGHEST)


def transform_cross(field, table_y, table_z):
    inner = jnp.einsum("ryz,zc->ryc", field, table_z, precision=lax.Precision.HIGHEST)
    return jnp.einsum("ryc,yb->rbc", inner, table_y, precision=lax.Precision.HIGHEST)


def body(source, reaction, conductance, coarse_inverse):
    block_x, block_y, block_z = source.shape
    extended = block_x + 2 * W
    padded_cond = with_halo(conductance, (("wide", 0), ("narrow", 1)), 1)
    face_x, face_y, face_z = face_weights(padded_cond, conductance)
    table_x, eigen_x = sine_basis(extended)
    table_y, eigen_y = sine_basis(block_y)
    table_z, eigen_z = sine_basis(block_z)
    spectrum = SHIFT + KAPPA * (
        eigen_x[:, None, None] + eigen_y[None, :, None] + eigen_z[None, None, :]
    )
    coarse_rows = coarse_inverse.reshape(PRIMAL, -1)

    def widen(field):
        return with_halo(field, (("wide", 0),), W)

    def fold_back(solved):
        owned = solved[W : W + block_x]
        for offset in (1, -1):
            rim_piece = solved[W + block_x :] if offset == 1 else solved[:W]
            arrived = passed_along(rim_piece, "wide", offset)
            if offset == 1:
                owned = owned + jnp.pad(arrived, ((0, block_x - W), (0, 0), (0, 0)))
            else:
                owned = owned + jnp.pad(arrived, ((block_x - W, 0), (0, 0), (0, 0)))
        return owned

    def precondition(field):
        coeffs = (
            transform_cross(transform_first(widen(field), table_x), table_y, table_z) / spectrum
        )
        local_part = fold_back(transform_cross(transform_first(coeffs, table_x), table_y, table_z))
        octant_means = (
            field.reshape(2, block_x // 2, 2, block_y // 2, 2, block_z // 2)
            .mean(axis=(1, 3, 5))
            .reshape(PRIMAL)
        )
        all_means = lax.all_gather(octant_means, ("wide", "narrow"), axis=0, tiled=True)
        correction = jnp.dot(coarse_rows, all_means, precision=lax.Precision.HIGHEST).reshape(
            2, 2, 2
        )
        spread = jnp.broadcast_to(
            correction[:, None, :, None, :, None],
            (2, block_x // 2, 2, block_y // 2, 2, block_z // 2),
        )
        return local_part + spread.reshape(block_x, block_y, block_z)

    def inner_norm(residual, preconditioned):
        return lax.psum(jnp.sum(residual * preconditioned), ("wide", "narrow"))

    solution = jnp.zeros_like(source)
    residual = source
    preconditioned = precondition(residual)
    direction = preconditioned
    gamma_now = inner_norm(residual, preconditioned)
    for iteration in range(ITERS):
        padded_field = with_halo(direction, (("wide", 0), ("narrow", 1)), 1)
        image = operate(direction, padded_field, reaction, face_x, face_y, face_z)
        step_size = gamma_now / lax.psum(jnp.sum(direction * image), ("wide", "narrow"))
        solution = solution + step_size * direction
        residual = residual - step_size * image
        preconditioned = precondition(residual)
        gamma_next = inner_norm(residual, preconditioned)
        direction = preconditioned + gamma_next / gamma_now * direction
        gamma_now = gamma_next
    return (solution, residual, direction)


def solution(mesh):
    in_specs = (
        P("wide", "narrow", None),
        P("wide", "narrow", None),
        P("wide", "narrow", None),
        P("wide", "narrow", None, None),
    )
    out_specs = (P("wide", "narrow", None), P("wide", "narrow", None), P("wide", "narrow", None))
    return jax.shard_map(body, mesh=mesh, in_specs=in_specs, out_specs=out_specs, check_vma=False)
```

profile of v0, /device:TPU:0, one launch (start us, length us, event | category | flops | bytes accessed | tf_op | source)
XLA Modules:
  0.0 502.6 jit_solution(13577779355339414686)
XLA Ops:
  3.4 3.8 collective-permute-start
  7.2 3.8 collective-permute-start.4
  18.0 41.9 %all-reduce.10 = f32[256]{0:T(256)S(1)} all-reduce(f32[256]{0:T(256)S(1)} %dynamic-update-slice), channel_id=1, replica_groups=mesh['wide'=8,'narrow'=4] {'wide','narrow'}, use_global_device_ids=true, to_apply=%add.10 | all-reduce | flops 256 | bytes 2048
  62.1 3.8 reshape.123
  70.9 3.7 fusion.20
  76.8 3.4 fusion.2
  80.3 3.7 fusion.17
  92.1 4.8 collective-permute-start.8
  98.7 4.0 collective-permute-start.7
  103.5 4.5 collective-permute-start.11
  110.2 3.6 collective-permute-done.10
  117.0 43.1 %all-reduce.13 = (f32[]{:T(128)}, f32[]{:T(128)}) all-reduce(f32[]{:T(128)} %get-tuple-element.4, f32[]{:T(128)} %get-tuple-element.3), channel_id=1, replica_groups=mesh['wide'=8,'narrow'=4] {'wide','narrow'}, use_global_device_ids=true, to_apply=%region_2.3 | all-reduce | flops 2 | bytes 16 | tf_op jit(solution)/shard_map/psum | solution.py:130
  164.3 3.5 collective-permute-start.12
  172.1 3.7 fusion.13
  178.0 3.4 fusion.1
  181.4 3.7 fusion.10
  185.1 3.5 convolution_bitcast_fusion.1
  192.2 8.5 %collective-permute-start.14 = (f32[8,128,128]{2,1,0:T(8,128)}, f32[8,128,128]{2,1,0:T(8,128)}, u32[]{:S(2)}, u32[]{:S(2)}) collective-permute-start(f32[8,128,128]{2,1,0:T(8,128)} %get-tuple-element.12), channel_id=1, source_target_pairs={{0,4},{4,8},{8,12},{12,16},{16,20},{20,24},{24,28},{1,5},{5,9},{9,... | collective-permute-start | bytes 1572872 | tf_op jit(solution)/shard_map/ppermute | solution.py:31
  206.3 42.0 %all-reduce.11 = f32[256]{0:T(256)S(1)} all-reduce(f32[256]{0:T(256)S(1)} %dynamic-update-slice.1), channel_id=1, replica_groups=mesh['wide'=8,'narrow'=4] {'wide','narrow'}, use_global_device_ids=true, to_apply=%add.11 | all-reduce | flops 256 | bytes 2048
  255.9 40.5 %psum.37 = f32[]{:T(128)} all-reduce(f32[]{:T(128)} %multiply_reduce_fusion.2), channel_id=1, replica_groups=mesh['wide'=8,'narrow'=4] {'wide','narrow'}, use_global_device_ids=true, to_apply=%region_7.8 | all-reduce | flops 1 | bytes 8 | tf_op jit(solution)/shard_map/psum | solution.py:130
  305.4 4.2 collective-permute-start.19
  311.8 3.7 collective-permute-done.18
  318.6 41.8 %psum.38 = f32[]{:T(128)} all-reduce(f32[]{:T(128)} %get-tuple-element.7), channel_id=1, replica_groups=mesh['wide'=8,'narrow'=4] {'wide','narrow'}, use_global_device_ids=true, to_apply=%region_9.10 | all-reduce | flops 1 | bytes 8 | tf_op jit(solution)/shard_map/psum | solution.py:140
  364.5 3.5 collective-permute-start.20
  372.4 3.7 fusion.6
  378.3 3.4 fusion
  381.7 3.7 fusion.3
  385.4 3.5 convolution_bitcast_fusion
  392.6 8.5 %collective-permute-start.22 = (f32[8,128,128]{2,1,0:T(8,128)}, f32[8,128,128]{2,1,0:T(8,128)}, u32[]{:S(2)}, u32[]{:S(2)}) collective-permute-start(f32[8,128,128]{2,1,0:T(8,128)} %get-tuple-element.10), channel_id=1, source_target_pairs={{0,4},{4,8},{8,12},{12,16},{16,20},{20,24},{24,28},{1,5},{5,9},{9,... | collective-permute-start | bytes 1572872 | tf_op jit(solution)/shard_map/ppermute | solution.py:31
  406.7 42.2 %all-reduce.12 = f32[256]{0:T(256)S(1)} all-reduce(f32[256]{0:T(256)S(1)} %dynamic-update-slice.2), channel_id=1, replica_groups=mesh['wide'=8,'narrow'=4] {'wide','narrow'}, use_global_device_ids=true, to_apply=%add.12 | all-reduce | flops 256 | bytes 2048
  457.2 40.2 %psum.39 = f32[]{:T(128)} all-reduce(f32[]{:T(128)} %multiply_reduce_fusion), channel_id=1, replica_groups=mesh['wide'=8,'narrow'=4] {'wide','narrow'}, use_global_device_ids=true, to_apply=%region_12.13 | all-reduce | flops 1 | bytes 8 | tf_op jit(solution)/shard_map/psum | solution.py:130
  498.8 3.6 multiply_add_fusion
  (136 shorter events, 100.6 us)
Async XLA Ops:
  0.6 11.7 %copy-start.4 = (f32[16,128,128]{2,1,0:T(8,128)S(1)}, f32[16,128,128]{2,1,0:T(8,128)}, u32[]{:S(2)}) copy-start(f32[16,128,128]{2,1,0:T(8,128)} %param.4) | copy-start | bytes 3145732
  2.1 64.4 %collective-permute-start.1 = (f32[8,128,128]{2,1,0:T(8,128)S(1)}, f32[8,128,128]{2,1,0:T(8,128)}, u32[]{:S(2)}, u32[]{:S(2)}) collective-permute-start(f32[8,128,128]{2,1,0:T(8,128)S(1)} %get-tuple-element.38), channel_id=1, source_target_pairs={{4,0},{8,4},{12,8},{16,12},{20,16},{24,20},{28,24},{5,1},{9,5},{13... | collective-permute-start | bytes 1572872 | tf_op jit(solution)/shard_map/ppermute | solution.py:23
  3.4 63.1 %collective-permute-start = (f32[8,128,128]{2,1,0:T(8,128)S(1)}, f32[8,128,128]{2,1,0:T(8,128)}, u32[]{:S(2)}, u32[]{:S(2)}) collective-permute-start(f32[8,128,128]{2,1,0:T(8,128)S(1)} %get-tuple-element.37), channel_id=1, source_target_pairs={{0,4},{4,8},{8,12},{12,16},{16,20},{20,24},{24,28},{1,5},{5,9},{9,... | collective-permute-start | bytes 1572872 | tf_op jit(solution)/shard_map/ppermute | solution.py:20
  7.2 58.8 %collective-permute-start.4 = (f32[1,128,128]{2,1,0:T(8,128)S(1)}, f32[1,128,128]{2,1,0:T(8,128)S(1)}, u32[]{:S(2)}, u32[]{:S(2)}) collective-permute-start(f32[1,128,128]{2,1,0:T(8,128)S(1)} %get-tuple-element.34), channel_id=1, source_target_pairs={{0,4},{4,8},{8,12},{12,16},{16,20},{20,24},{24,28},{1,5},{5,9},{9,... | collective-permute-start | bytes 196616 | tf_op jit(solution)/shard_map/ppermute | solution.py:20
  11.0 48.8 %copy-start.14 = (f32[1,1,8,256]{3,2,1,0:T(8,128)S(1)}, f32[1,1,8,256]{3,2,1,0:T(8,128)}, u32[]{:S(2)}) copy-start(f32[1,1,8,256]{3,2,1,0:T(8,128)} %param.7) | copy-start | bytes 24580
  11.0 55.4 %collective-permute-start.5 = (f32[1,128,128]{2,1,0:T(8,128)S(1)}, f32[1,128,128]{2,1,0:T(8,128)S(1)}, u32[]{:S(2)}, u32[]{:S(2)}) collective-permute-start(f32[1,128,128]{2,1,0:T(8,128)S(1)} %get-tuple-element.33), channel_id=1, source_target_pairs={{4,0},{8,4},{12,8},{16,12},{20,16},{24,20},{28,24},{5,1},{9,5},{13... | collective-permute-start | bytes 196616 | tf_op jit(solution)/shard_map/ppermute | solution.py:23
  86.3 10.9 %copy-start.11 = (f32[16,128,128]{2,1,0:T(8,128)S(1)}, f32[16,128,128]{2,1,0:T(8,128)}, u32[]{:S(2)}) copy-start(f32[16,128,128]{2,1,0:T(8,128)} %reshape.123) | copy-start | bytes 3145732
  86.3 10.9 %collective-permute-start.3 = (f32[8,128,128]{2,1,0:T(8,128)S(1)}, f32[8,128,128]{2,1,0:T(8,128)S(1)}, u32[]{:S(2)}, u32[]{:S(2)}) collective-permute-start(f32[8,128,128]{2,1,0:T(8,128)S(1)} %get-tuple-element.15), channel_id=1, source_target_pairs={{4,0},{8,4},{12,8},{16,12},{20,16},{24,20},{28,24},{5,1},{9,5},{13... | collective-permute-start | bytes 1572872 | tf_op jit(solution)/shard_map/ppermute | solution.py:31
  87.7 9.4 %collective-permute-start.2 = (f32[8,128,128]{2,1,0:T(8,128)S(1)}, f32[8,128,128]{2,1,0:T(8,128)S(1)}, u32[]{:S(2)}, u32[]{:S(2)}) collective-permute-start(f32[8,128,128]{2,1,0:T(8,128)S(1)} %get-tuple-element.14), channel_id=1, source_target_pairs={{0,4},{4,8},{8,12},{12,16},{16,20},{20,24},{24,28},{1,5},{5,9},{9,... | collective-permute-start | bytes 1572872 | tf_op jit(solution)/shard_map/ppermute | solution.py:31
  90.8 11.8 %collective-permute-start.9 = (f32[18,1,128]{2,1,0:T(1,128)S(1)}, f32[18,1,128]{2,1,0:T(1,128)S(1)}, u32[]{:S(2)}, u32[]{:S(2)}) collective-permute-start(f32[18,1,128]{2,1,0:T(1,128)S(1)} %get-tuple-element.21), channel_id=1, source_target_pairs={{1,0},{2,1},{3,2},{5,4},{6,5},{7,6},{9,8},{10,9},{11,10},{13,12},{... | collective-permute-start | bytes 27656 | tf_op jit(solution)/shard_map/ppermute | solution.py:23
  92.1 10.6 %collective-permute-start.8 = (f32[18,1,128]{2,1,0:T(1,128)S(1)}, f32[18,1,128]{2,1,0:T(1,128)S(1)}, u32[]{:S(2)}, u32[]{:S(2)}) collective-permute-start(f32[18,1,128]{2,1,0:T(1,128)S(1)} %get-tuple-element.20), channel_id=1, source_target_pairs={{0,1},{1,2},{2,3},{4,5},{5,6},{6,7},{8,9},{9,10},{10,11},{12,13},{... | collective-permute-start | bytes 27656 | tf_op jit(solution)/shard_map/ppermute | solution.py:20
  97.1 16.7 %copy-start.6 = (f32[17,128,128]{2,1,0:T(8,128)}, f32[17,128,128]{2,1,0:T(8,128)S(1)}, u32[]{:S(2)}) copy-start(f32[17,128,128]{2,1,0:T(8,128)S(1)} %add_divide_fusion.1) | copy-start | bytes 3342340
  97.4 5.6 %collective-permute-start.6 = (f32[1,128,128]{2,1,0:T(8,128)S(1)}, f32[1,128,128]{2,1,0:T(8,128)S(1)}, u32[]{:S(2)}, u32[]{:S(2)}) collective-permute-start(f32[1,128,128]{2,1,0:T(8,128)S(1)} %get-tuple-element.36), channel_id=1, source_target_pairs={{4,0},{8,4},{12,8},{16,12},{20,16},{24,20},{28,24},{5,1},{9,5},{13... | collective-permute-start | bytes 196616 | tf_op jit(solution)/shard_map/ppermute | solution.py:23
  98.7 4.9 collective-permute-start.7
  103.5 6.6 %collective-permute-start.11 = (f32[18,1,128]{2,1,0:T(1,128)S(1)}, f32[18,1,128]{2,1,0:T(1,128)S(1)}, u32[]{:S(2)}, u32[]{:S(2)}) collective-permute-start(f32[18,1,128]{2,1,0:T(1,128)S(1)} %get-tuple-element.19), channel_id=1, source_target_pairs={{0,1},{1,2},{2,3},{4,5},{5,6},{6,7},{8,9},{9,10},{10,11},{12,13},{... | collective-permute-start | bytes 27656 | tf_op jit(solution)/shard_map/ppermute | solution.py:20
  108.1 5.7 %collective-permute-start.10 = (f32[18,1,128]{2,1,0:T(1,128)S(1)}, f32[18,1,128]{2,1,0:T(1,128)S(1)}, u32[]{:S(2)}, u32[]{:S(2)}) collective-permute-start(f32[18,1,128]{2,1,0:T(1,128)S(1)} %get-tuple-element.18), channel_id=1, source_target_pairs={{1,0},{2,1},{3,2},{5,4},{6,5},{7,6},{9,8},{10,9},{11,10},{13,12},{... | collective-permute-start | bytes 27656 | tf_op jit(solution)/shard_map/ppermute | solution.py:23
  110.1 51.4 %copy-start.5 = (f32[16,128,128]{2,1,0:T(8,128)S(1)}, f32[16,128,128]{2,1,0:T(8,128)}, u32[]{:S(2)}) copy-start(f32[16,128,128]{2,1,0:T(8,128)} %param.4) | copy-start | bytes 3145732
  163.0 4.8 collective-permute-start.13
  164.3 4.6 collective-permute-start.12
  190.9 62.2 %collective-permute-start.15 = (f32[8,128,128]{2,1,0:T(8,128)}, f32[8,128,128]{2,1,0:T(8,128)}, u32[]{:S(2)}, u32[]{:S(2)}) collective-permute-start(f32[8,128,128]{2,1,0:T(8,128)} %get-tuple-element.13), channel_id=1, source_target_pairs={{4,0},{8,4},{12,8},{16,12},{20,16},{24,20},{28,24},{5,1},{9,5},{13... | collective-permute-start | bytes 1572872 | tf_op jit(solution)/shard_map/ppermute | solution.py:31
  192.2 60.9 %collective-permute-start.14 = (f32[8,128,128]{2,1,0:T(8,128)}, f32[8,128,128]{2,1,0:T(8,128)}, u32[]{:S(2)}, u32[]{:S(2)}) collective-permute-start(f32[8,128,128]{2,1,0:T(8,128)} %get-tuple-element.12), channel_id=1, source_target_pairs={{0,4},{4,8},{8,12},{12,16},{16,20},{20,24},{24,28},{1,5},{5,9},{9,... | collective-permute-start | bytes 1572872 | tf_op jit(solution)/shard_map/ppermute | solution.py:31
  253.1 43.3 %copy-start.10 = (f32[16,128,128]{2,1,0:T(8,128)}, f32[16,128,128]{2,1,0:T(8,128)S(1)}, u32[]{:S(2)}) copy-start(f32[16,128,128]{2,1,0:T(8,128)S(1)} %reshape.125) | copy-start | bytes 3145732
  297.9 13.3 %copy-start.1 = (f32[16,128,128]{2,1,0:T(8,128)S(1)}, f32[16,128,128]{2,1,0:T(8,128)}, u32[]{:S(2)}) copy-start(f32[16,128,128]{2,1,0:T(8,128)} %param.6) | copy-start | bytes 3145732
  300.1 4.3 collective-permute-start.16
  301.4 3.9 collective-permute-start.17
  305.4 6.4 %collective-permute-start.19 = (f32[18,1,128]{2,1,0:T(1,128)S(1)}, f32[18,1,128]{2,1,0:T(1,128)S(1)}, u32[]{:S(2)}, u32[]{:S(2)}) collective-permute-start(f32[18,1,128]{2,1,0:T(1,128)S(1)} %get-tuple-element.17), channel_id=1, source_target_pairs={{0,1},{1,2},{2,3},{4,5},{5,6},{6,7},{8,9},{9,10},{10,11},{12,13},{... | collective-permute-start | bytes 27656 | tf_op jit(solution)/shard_map/ppermute | solution.py:20
  309.6 5.9 %collective-permute-start.18 = (f32[18,1,128]{2,1,0:T(1,128)S(1)}, f32[18,1,128]{2,1,0:T(1,128)S(1)}, u32[]{:S(2)}, u32[]{:S(2)}) collective-permute-start(f32[18,1,128]{2,1,0:T(1,128)S(1)} %get-tuple-element.16), channel_id=1, source_target_pairs={{1,0},{2,1},{3,2},{5,4},{6,5},{7,6},{9,8},{10,9},{11,10},{13,12},{... | collective-permute-start | bytes 27656 | tf_op jit(solution)/shard_map/ppermute | solution.py:23
  363.2 4.8 collective-permute-start.21
  364.5 4.6 collective-permute-start.20
  388.9 12.2 %copy-start.3 = (f32[16,128,128]{2,1,0:T(8,128)S(1)}, f32[16,128,128]{2,1,0:T(8,128)}, u32[]{:S(2)}) copy-start(f32[16,128,128]{2,1,0:T(8,128)} %copy-done.2) | copy-start | bytes 3145732
  391.3 63.2 %collective-permute-start.23 = (f32[8,128,128]{2,1,0:T(8,128)}, f32[8,128,128]{2,1,0:T(8,128)}, u32[]{:S(2)}, u32[]{:S(2)}) collective-permute-start(f32[8,128,128]{2,1,0:T(8,128)} %get-tuple-element.11), channel_id=1, source_target_pairs={{4,0},{8,4},{12,8},{16,12},{20,16},{24,20},{28,24},{5,1},{9,5},{13... | collective-permute-start | bytes 1572872 | tf_op jit(solution)/shard_map/ppermute | solution.py:31
  392.6 61.9 %collective-permute-start.22 = (f32[8,128,128]{2,1,0:T(8,128)}, f32[8,128,128]{2,1,0:T(8,128)}, u32[]{:S(2)}, u32[]{:S(2)}) collective-permute-start(f32[8,128,128]{2,1,0:T(8,128)} %get-tuple-element.10), channel_id=1, source_target_pairs={{0,4},{4,8},{8,12},{12,16},{16,20},{20,24},{24,28},{1,5},{5,9},{9,... | collective-permute-start | bytes 1572872 | tf_op jit(solution)/shard_map/ppermute | solution.py:31
  (7 other events, 47.1 us)
where the time goes:
time: 509 us; the launch traced here: 503 us
  blocking collectives  292 us (57%)
  starting transfers between devices  71.2 us (14%)
  matrix products  58.4 us (11%)
  other arithmetic  32.5 us (6%)
  local copies, waits for them, and re-layouts  30.7 us (6%)
  waiting for transfers between devices  10.9 us (2%)
  between operations  7.15 us (1%)
    unnamed x3, blocking collectives  126 us
    psum x3, blocking collectives, inner_norm(): return lax.psum(jnp.sum(residual * preconditioned), ('wide', 'narrow'))  124 us
    psum x1, blocking collectives, body(): lax.psum(jnp.sum(direction * image), ('wide', 'narrow'))  41.8 us
    ppermute x9, starting transfers between devices, with_halo(): lax.ppermute(lax.slice_in_dim(block, block.shape[dim] - width, None, axis...  35.1 us
    ppermute x6, starting transfers between devices, passed_along(): return lax.ppermute(block, axis, route)  24.1 us
    dot_general x6, matrix products, transform_cross(): jnp.einsum('ryz,zc->ryc', field, table_z, precision=lax.Precision.HIGHEST)  22 us
    dot_general x6, matrix products, transform_first(): jnp.einsum('ryz,re->eyz', field, table_x, precision=lax.Precision.HIGHEST)  19.6 us
    dot_general x6, matrix products, transform_cross(): jnp.einsum('ryc,yb->rbc', inner, table_y, precision=lax.Precision.HIGHEST)  15.9 us
  transfers between devices with their start and end apart: 24, of which 6 were waited for; matrix products, arithmetic and copies ran while one was open for 7% of the time, Pallas kernels for 0%

commit v1 on v0

v1 whole, which is shorter than its diff:
```python
import functools

import jax
import jax.numpy as jnp
import numpy as np
from jax import lax
from jax.experimental import pallas as pl
from jax.experimental.pallas import tpu as pltpu
from jax.sharding import PartitionSpec as P

W = 8
PRIMAL = 8
SHIFT = 0.06
MESH = pl.DeviceIdType.MESH
f32 = jnp.float32
bf16 = jnp.bfloat16


def sine_basis(extent):
    indices = np.arange(extent, dtype=np.float64) + 1.0
    angles = np.pi * indices[:, None] * indices[None, :] / (extent + 1)
    table = np.sqrt(2.0 / (extent + 1)) * np.sin(angles)
    eigen = 2.0 - 2.0 * np.cos(np.pi * indices / (extent + 1))
    return table, eigen


def split(value):
    high = value.astype(bf16)
    return high, (value - high.astype(f32)).astype(bf16)


def harmonic(first, second):
    return 2.0 * first * second / (first + second)


def kernel(
    nw, nn, src, rea, con, cexp, tabz, taby, eigy, eigz, x_out, r_out, d_out,
    spec_r, spec_w0, spec_w1, own, total, tail, head, cp, inv, fx, fy, fylo, fz,
    z0, z1, w0, w1, chx, chy, cys, pqs, pqr, yr, hx, hy, hys, ga, gb, gc, gd,
    nsend, nrecv, gs1, gr1, gs2, gr2,
):
    bx, by, bz = src.shape
    iw, inn = lax.axis_index("wide"), lax.axis_index("narrow")
    place = {"wide": (iw, nw), "narrow": (inn, nn)}

    barrier = pltpu.get_barrier_semaphore()

    def greet(axis):
        me, count = place[axis]

        def one(k, carry):
            pl.semaphore_signal(
                barrier, inc=1, device_id={axis: lax.rem(me + k, count)}, device_id_type=MESH
            )
            return carry

        lax.fori_loop(1, count, one, 0)

    greet("wide")
    greet("narrow")
    pl.semaphore_wait(barrier, nw + nn - 2)

    class Shift:
        def __init__(self, source, target, slot, axis, step):
            me, count = place[axis]
            if step > 0:
                self.sends, self.gets = me < count - 1, me > 0
            else:
                self.sends, self.gets = me > 0, me < count - 1
            self.copy = pltpu.make_async_remote_copy(
                src_ref=source, dst_ref=target, send_sem=nsend.at[slot], recv_sem=nrecv.at[slot],
                device_id={axis: me + step}, device_id_type=MESH,
            )

        def start(self):
            @pl.when(self.sends)
            def _():
                self.copy.start()

        def arrive(self):
            @pl.when(self.gets)
            def _():
                self.copy.wait_recv()

        def leave(self):
            @pl.when(self.sends)
            def _():
                self.copy.wait_send()

    def pair(low_source, high_source, target, slot, axis):
        return (
            Shift(high_source, target.at[0], slot, axis, 1),
            Shift(low_source, target.at[1], slot + 1, axis, -1),
        )

    def each(copies, verb):
        for copy in copies:
            getattr(copy, verb)()

    class Gather:
        def __init__(self, ref, slot):
            self.ref, self.slot = ref, slot

        def near(self, k):
            return pltpu.make_async_remote_copy(
                src_ref=self.ref.at[iw, inn], dst_ref=self.ref.at[iw, inn],
                send_sem=gs1.at[self.slot, k], recv_sem=gr1.at[self.slot, k],
                device_id={"narrow": lax.rem(inn + k, nn)}, device_id_type=MESH,
            )

        def far(self, k):
            return pltpu.make_async_remote_copy(
                src_ref=self.ref.at[iw], dst_ref=self.ref.at[iw],
                send_sem=gs2.at[self.slot, k], recv_sem=gr2.at[self.slot, k],
                device_id={"wide": lax.rem(iw + k, nw)}, device_id_type=MESH,
            )

        def loop(self, count, step):
            def one(k, carry):
                step(k)
                return carry

            lax.fori_loop(1, count, one, 0)

        def first(self):
            self.loop(nn, lambda k: self.near(k).start())

        def second(self):
            self.loop(nn, lambda k: self.near(k).wait())
            self.loop(nw, lambda k: self.far(k).start())

        def finish(self):
            self.loop(nw, lambda k: self.far(k).wait())

    for edge, side in ((iw == 0, 0), (iw == nw - 1, 1)):
        @pl.when(edge)
        def _():
            blank = jnp.zeros((by, bz), f32)
            chx[side] = blank
            for turn in range(3):
                pqr[turn, side] = blank
                yr[turn, side] = blank
            for turn in range(2):
                hx[turn, side] = blank

    for edge, side in ((inn == 0, 0), (inn == nn - 1, 1)):
        @pl.when(edge)
        def _():
            blank = jnp.zeros((bx, bz), f32)
            chy[side] = blank
            for turn in range(2):
                hy[turn, side] = blank

    cys[0] = con[:, 0, :]
    cys[1] = con[:, by - 1, :]
    cond_x = pair(con.at[0], con.at[bx - 1], chx, 0, "wide")
    cond_y = pair(cys.at[0], cys.at[1], chy, 2, "narrow")
    each(cond_x + cond_y, "start")

    def fold8(value):
        return value.reshape(value.shape[0] // 8, 8, bz).sum(axis=0)

    half_y, half_x = by // 2, bx // 2
    zero8 = jnp.zeros((8, bz), f32)

    def post(ref, rows):
        for k, row in enumerate(rows):
            ref[iw, inn, pl.ds(k, 1), :] = jnp.sum(row, axis=0, keepdims=True)

    def means_of(field):
        rows = []
        for part in range(2):
            def one(x, carry):
                value = field[x]
                return carry[0] + fold8(value[:half_y]), carry[1] + fold8(value[half_y:])

            rows += list(lax.fori_loop(part * half_x, (part + 1) * half_x, one, (zero8, zero8)))
        return rows

    gather_a, gather_b, gather_c, gather_d = (
        Gather(ref, slot) for slot, ref in enumerate((ga, gb, gc, gd))
    )
    post(ga, means_of(src) + [zero8] * 4)
    gather_a.first()

    def along_z(value):
        high, low = split(value)
        both = jnp.dot(
            jnp.concatenate([high, low], axis=1), tabz[...], preferred_element_type=f32
        )
        return both[:, :bz] + both[:, bz:]

    def along_y(value):
        high, low = split(value)
        pairs = jnp.concatenate([high, low], axis=1)
        both = jnp.dot(
            taby[...], jnp.concatenate([pairs, pairs], axis=0), preferred_element_type=f32
        )
        return both[:, :bz] + both[:, bz:]

    step = 4

    def forward(field, out):
        def one(k, carry):
            rows = pl.ds(k * step, step)
            value = along_z(field[rows].reshape(step * by, bz))
            for j in range(step):
                out[k * step + j] = along_y(value[j * by : (j + 1) * by])
            return carry

        lax.fori_loop(0, bx // step, one, 0)

    chunk = by // 2
    on_left = (iw > 0).astype(f32)
    on_right = (iw < nw - 1).astype(f32)

    def chunks(work):
        def one(k, carry):
            work(pl.ds(pl.multiple_of(k * chunk, chunk), chunk))
            return carry

        lax.fori_loop(0, by // chunk, one, 0)

    def eliminate(rows):
        diagonal = 2.0 + SHIFT + eigy[rows, :] + eigz[...]
        last = 1.0 / diagonal
        cp[0, rows, :] = last
        for k in range(1, W + bx):
            last = 1.0 / (diagonal - last)
            cp[k, rows, :] = last
        inv[rows, :] = 1.0 / (1.0 - last * cp[W - 1, rows, :])

    chunks(eliminate)

    def solve(turn, prepare):
        def ends(rows):
            prepare(rows)
            value = jnp.zeros((chunk, bz), f32)
            for k in range(W):
                value = (spec_r[bx - W + k, rows, :] + value) * cp[k, rows, :]
                tail[k, rows, :] = value
            pqs[turn, 1, rows, :] = value
            value = jnp.zeros((chunk, bz), f32)
            for t in reversed(range(W)):
                value = (spec_r[t, rows, :] + value) * cp[W - 1 - t, rows, :]
                head[t, rows, :] = value
            pqs[turn, 0, rows, :] = value

        chunks(ends)
        rims = pair(pqs.at[turn, 0], pqs.at[turn, 1], pqr.at[turn], 4 + 4 * turn, "wide")
        each(rims, "start")
        yield
        each(rims, "arrive")

        def middle(rows):
            value = pqr[turn, 0, rows, :]
            for t in range(bx):
                value = (spec_r[t, rows, :] + value) * cp[W + t, rows, :]
                if t < bx - 1:
                    own[t, rows, :] = value
            value = (value + cp[W + bx - 1, rows, :] * pqr[turn, 1, rows, :]) * inv[rows, :]
            own[bx - 1, rows, :] = value
            for t in reversed(range(bx - 1)):
                value = own[t, rows, :] + cp[W + t, rows, :] * value
                own[t, rows, :] = value

        chunks(middle)
        backs = pair(own.at[0], own.at[bx - 1], yr.at[turn], 6 + 4 * turn, "wide")
        each(backs, "start")
        yield
        each(backs, "arrive")

        def fold(rows):
            value = yr[turn, 1, rows, :]
            for k in reversed(range(W)):
                value = tail[k, rows, :] + cp[k, rows, :] * value
                t = bx - W + k
                total[t, rows, :] = own[t, rows, :] + on_right * value
            value = yr[turn, 0, rows, :]
            for t in range(W):
                value = head[t, rows, :] + cp[W - 1 - t, rows, :] * value
                total[t, rows, :] = own[t, rows, :] + on_left * value

        chunks(fold)
        each(rims, "leave")
        each(backs, "leave")
        yield

    lanes = lax.broadcasted_iota(jnp.int32, (1, bz), 1)

    def inverse(correction, out):
        for part in range(2):
            spread = []
            for side in range(2):
                o = part * 4 + side * 2
                row = jnp.where(lanes < bz // 2, correction[o], correction[o + 1])
                spread.append(jnp.broadcast_to(row, (half_y, bz)))
            spread = jnp.concatenate(spread, axis=0)

            def one(k, carry):
                value = jnp.concatenate(
                    [along_y(total[k * step + j]) for j in range(step)], axis=0
                )
                value = along_z(value)
                for j in range(step):
                    out[k * step + j] = value[j * by : (j + 1) * by] + spread
                return carry

            lax.fori_loop(part * (half_x // step), (part + 1) * (half_x // step), one, 0)

    scale = 1.0 / (half_x * half_y * (bz // 2))

    def everything(value):
        return jnp.sum(jnp.sum(value, axis=0, keepdims=True), axis=1, keepdims=True)

    def correct(ref):
        message = ref[...].reshape(nw * nn, 8, bz)
        return [everything(jnp.sum(message * cexp[o], axis=0)) * scale for o in range(PRIMAL)]

    def dots(ref):
        whole = jnp.sum(ref[...].reshape(nw * nn, 8, bz), axis=0)
        return [jnp.sum(whole[k : k + 1], axis=1, keepdims=True) for k in range(4, 7)]

    index_y = lax.broadcasted_iota(jnp.int32, (by, bz), 0)

    def shifted_down(value, low):
        return jnp.where(index_y == 0, low, pltpu.roll(value, 1, 0))

    def shifted_up(value, high):
        return jnp.where(index_y == by - 1, high, pltpu.roll(value, by - 1, 0))

    def weights():
        each(cond_x + cond_y, "arrive")
        index_z = lax.broadcasted_iota(jnp.int32, (by, bz), 1)
        fx[0] = harmonic(chx[0], con[0])
        fx[bx] = harmonic(con[bx - 1], chx[1])

        def one(x, carry):
            value = con[x]
            fy[x] = harmonic(value, shifted_up(value, chy[1, pl.ds(x, 1), :]))
            fz[x] = jnp.where(
                index_z == bz - 1, 0.0, harmonic(value, pltpu.roll(value, bz - 1, 1))
            )
            return carry

        def between(x, carry):
            fx[x] = harmonic(con[x - 1], con[x])
            return carry

        lax.fori_loop(0, bx, one, 0)
        lax.fori_loop(1, bx, between, 0)
        fylo[...] = harmonic(cys[0], chy[0])
        each(cond_x + cond_y, "leave")

    def apply(turn, field, out, inner):
        hys[turn, 0] = field[:, 0, :]
        hys[turn, 1] = field[:, by - 1, :]
        slot = 16 + 4 * turn
        layers = pair(field.at[0], field.at[bx - 1], hx.at[turn], slot, "wide") + pair(
            hys.at[turn, 0], hys.at[turn, 1], hy.at[turn], slot + 2, "narrow"
        )
        each(layers, "start")
        if turn == 0:
            weights()
        each(layers, "arrive")

        def point(x, below, above):
            value = field[x]
            result = rea[x] * value
            result = result + fx[x + 1] * (value - above) + fx[x] * (value - below)
            flux = fy[x] * (value - shifted_up(value, hy[turn, 1, pl.ds(x, 1), :]))
            low = fylo[pl.ds(x, 1), :] * (hy[turn, 0, pl.ds(x, 1), :] - value[0:1])
            result = result + flux - shifted_down(flux, low)
            flux = fz[x] * (value - pltpu.roll(value, bz - 1, 1))
            result = result + flux - pltpu.roll(flux, 1, 1)
            out[x] = result
            return value, result

        sums, products = [], [zero8] * 3

        def gather_up(x, below, above, carry):
            value, result = point(x, below, above)
            extra = inner(x, value, result)
            return (
                carry[0] + fold8(result[:half_y]), carry[1] + fold8(result[half_y:]),
            ) + tuple(c + fold8(e) for c, e in zip(carry[2:], extra))

        for part in range(2):
            carry = (zero8, zero8) + tuple(products)
            if part == 0:
                carry = gather_up(0, hx[turn, 0], field[1], carry)
                low, high = 1, half_x
            else:
                low, high = half_x, bx - 1
            carry = lax.fori_loop(
                low, high, lambda x, c: gather_up(x, field[x - 1], field[x + 1], c), carry
            )
            if part == 1:
                carry = gather_up(bx - 1, field[bx - 2], hx[turn, 1], carry)
            sums += [carry[0], carry[1]]
            products = list(carry[2:])
        each(layers, "leave")
        return sums + products + [zero8]

    def local(turn, prepare, between=None):
        stages = solve(turn, prepare)
        next(stages)
        if between is not None:
            between()
        next(stages)
        next(stages)

    forward(src, spec_r)
    gather_a.second()
    local(0, lambda rows: None)
    gather_a.finish()
    coarse = correct(ga)
    inverse(coarse, z0)
    post(gb, apply(0, z0, w0, lambda x, v, a: (src[x] * v, v * a, zero8)))
    gather_b.first()

    forward(w0, spec_w0)
    gather_b.second()
    gather_b.finish()
    gamma0, delta0, _ = dots(gb)
    alpha0 = gamma0 / delta0

    def first_step(rows):
        for t in range(bx):
            spec_r[t, rows, :] = spec_r[t, rows, :] - alpha0 * spec_w0[t, rows, :]

    local(1, first_step)
    coarse_b = correct(gb)
    coarse = [a - alpha0 * b for a, b in zip(coarse, coarse_b)]
    inverse(coarse, z1)

    def inner(x, value, result):
        image = w0[x]
        return (src[x] - alpha0 * image) * value, value * result, value * image

    post(gc, apply(1, z1, w1, inner))
    gather_c.first()

    forward(w1, spec_w1)
    gather_c.second()
    gather_c.finish()
    gamma1, own1, cross1 = dots(gc)
    beta1 = gamma1 / gamma0
    alpha1 = gamma1 / (own1 + 2.0 * beta1 * cross1 + beta1 * beta1 * delta0)

    def second_step(rows):
        for t in range(bx):
            image = spec_w1[t, rows, :] + beta1 * spec_w0[t, rows, :]
            spec_r[t, rows, :] = spec_r[t, rows, :] - alpha1 * image

    def results():
        def one(x, carry):
            direction = z1[x] + beta1 * z0[x]
            x_out[x] = alpha0 * z0[x] + alpha1 * direction
            image = w0[x]
            r_out[x] = (src[x] - alpha0 * image) - alpha1 * (w1[x] + beta1 * image)
            z1[x] = direction
            return carry

        lax.fori_loop(0, bx, one, 0)

    local(2, second_step, results)
    coarse_c = correct(gc)
    coarse = [a - alpha1 * (c + beta1 * b) for a, b, c in zip(coarse, coarse_b, coarse_c)]
    inverse(coarse, w1)
    product = lax.fori_loop(0, bx, lambda x, c: c + fold8(r_out[x] * w1[x]), zero8)
    post(gd, [zero8] * 4 + [product] + [zero8] * 3)
    gather_d.first()
    gather_d.second()
    gather_d.finish()
    beta2 = dots(gd)[0] / gamma1

    def last(x, carry):
        d_out[x] = w1[x] + beta2 * z1[x]
        return carry

    lax.fori_loop(0, bx, last, 0)


def body(nw, nn, source, reaction, conductance, coarse_inverse):
    bx, by, bz = source.shape
    table_y, eigen_y = sine_basis(by)
    table_z, eigen_z = sine_basis(bz)

    def parts(table):
        table = np.asarray(table, np.float32)
        high = table.astype(jnp.bfloat16)
        low = (table - high.astype(np.float32)).astype(jnp.bfloat16)
        return np.concatenate([high, low], axis=1)

    tab_y = parts(table_y)
    tab_z = parts(table_z)
    tab_z = np.concatenate([tab_z, tab_z], axis=0)
    rows = coarse_inverse.reshape(PRIMAL, nw * nn, 4, 2, 1)
    rows = jnp.broadcast_to(rows, (PRIMAL, nw * nn, 4, 2, bz // 2)).reshape(
        PRIMAL, nw * nn, 4, bz
    )
    rows = jnp.pad(rows, ((0, 0), (0, 0), (0, 4), (0, 0)))
    block = (bx, by, bz)
    layer = (by, bz)

    def vm(*shape):
        return pltpu.VMEM(shape, f32)

    scratch = [
        vm(*block), vm(*block), vm(*block), vm(*block), vm(*block),
        vm(W, *layer), vm(W, *layer), vm(W + bx, *layer), vm(*layer),
        vm(bx + 1, *layer), vm(*block), vm(bx, bz), vm(*block),
        vm(*block), vm(*block), vm(*block), vm(*block),
        vm(2, *layer), vm(2, bx, bz), vm(2, bx, bz),
        vm(3, 2, *layer), vm(3, 2, *layer), vm(3, 2, *layer),
        vm(2, 2, *layer), vm(2, 2, bx, bz), vm(2, 2, bx, bz),
        vm(nw, nn, 8, bz), vm(nw, nn, 8, bz), vm(nw, nn, 8, bz), vm(nw, nn, 8, bz),
        pltpu.SemaphoreType.DMA((24,)), pltpu.SemaphoreType.DMA((24,)),
        pltpu.SemaphoreType.DMA((4, nn)), pltpu.SemaphoreType.DMA((4, nn)),
        pltpu.SemaphoreType.DMA((4, nw)), pltpu.SemaphoreType.DMA((4, nw)),
    ]
    spec = pl.BlockSpec(memory_space=pltpu.VMEM)
    return pl.pallas_call(
        functools.partial(kernel, nw, nn),
        out_shape=[jax.ShapeDtypeStruct(block, f32)] * 3,
        in_specs=[spec] * 8,
        out_specs=[spec] * 3,
        scratch_shapes=scratch,
        compiler_params=pltpu.CompilerParams(
            collective_id=0, has_side_effects=True, vmem_limit_bytes=52 * 1024 * 1024
        ),
    )(
        source, reaction, conductance, rows,
        jnp.asarray(tab_z), jnp.asarray(tab_y),
        jnp.asarray(eigen_y.reshape(-1, 1), f32), jnp.asarray(eigen_z.reshape(1, -1), f32),
    )


def solution(mesh):
    grid = P("wide", "narrow", None)
    return jax.shard_map(
        functools.partial(body, mesh.shape["wide"], mesh.shape["narrow"]),
        mesh=mesh,
        in_specs=(grid, grid, grid, P("wide", "narrow", None, None)),
        out_specs=(grid, grid, grid),
        check_vma=False,
    )
```

time: 509 us -> 82 us (0.16); the launches traced: 503 us -> 81.7 us
  blocking collectives: 292 us -> 0 us
  Pallas kernels: 0 us -> 72.1 us
  starting transfers between devices: 71.2 us -> 0 us
  matrix products: 58.4 us -> 0 us
  other arithmetic: 32.5 us -> 0 us
  local copies, waits for them, and re-layouts: 30.7 us -> 8.94 us
  waiting for transfers between devices: 10.9 us -> 0 us
  between operations: 7.15 us -> 0.71 us
    psum x4 -> x0, blocking collectives: 166 us -> none  [the longest x3 124 us: inner_norm(): return lax.psum(jnp.sum(residual * preconditioned), ('wide', 'narrow'))]
    unnamed x3 -> x0, blocking collectives: 126 us -> none
    pallas_call x0 -> x1, Pallas kernels: none -> 72.1 us  [body(): pl.pallas_call(functools.partial(kernel, nw, nn), out_shape=[jax.ShapeDty...]
    ppermute x24 -> x0, starting transfers between devices: 71.2 us -> none  [the longest x9 35.1 us: with_halo(): lax.ppermute(lax.slice_in_dim(block, block.shape[dim] - width, None, axis...]
    dot_general x21 -> x0, matrix products: 58.4 us -> none  [the longest x6 22 us: transform_cross(): jnp.einsum('ryz,zc->ryc', field, table_z, precision=lax.Precision.HIGHEST)]
    reduce_sum x7 -> x0, other arithmetic: 20.1 us -> none  [the longest x3 8.27 us: precondition(): octant_means = field.reshape(2, block_x // 2, 2, block_y // 2, 2, block_z...]
    reshape x6 -> x1, local copies, waits for them, and re-layouts: 17.2 us -> 0.76 us  [body(): jnp.broadcast_to(rows, (PRIMAL, nw * nn, 4, 2, bz // 2))]
    ppermute x24 -> x0, waiting for transfers between devices: 10.9 us -> none  [the longest x9 7.32 us: with_halo(): lax.ppermute(lax.slice_in_dim(block, 0, width, axis=dim), axis, backward)]
  transfers between devices with their start and end apart: 24 -> 0, of which waited for: 6 -> 0; matrix products, arithmetic and copies ran while one was open for 7% -> 0% of each run, Pallas kernels for 0% -> 0%
where the time goes in v1:
time: 82 us; the launch traced here: 81.7 us
  Pallas kernels  72.1 us (88%)
  local copies, waits for them, and re-layouts  8.94 us (11%)
    pallas_call x1, Pallas kernels, body(): pl.pallas_call(functools.partial(kernel, nw, nn), out_shape=[jax.ShapeDty...  72.1 us
    unnamed x16, local copies, waits for them, and re-layouts  5.01 us
    broadcast_in_dim x2, local copies, waits for them, and re-layouts, body(): jnp.broadcast_to(rows, (PRIMAL, nw * nn, 4, 2, bz // 2))  2.13 us

profile of v1, /device:TPU:0, one launch (start us, length us, event | category | flops | bytes accessed | tf_op | source)
XLA Modules:
  0.0 81.7 jit_solution(1078020289513032882)
XLA Ops:
  0.6 0.8 %copy.11 = f32[1,1,8,256]{2,3,1,0:T(8,128)S(1)} copy(f32[1,1,8,256]{3,2,1,0:T(8,128)} %param.11) | data formatting | bytes 16384 | tf_op args[3]
  1.5 0.9 %copy.12 = f32[8,32,4,2]{3,2,1,0:T(4,128)S(1)} copy(f32[8,32,4,2]{0,3,2,1:T(2,128)S(1)} %bitcast.1) | data formatting | bytes 16384 | tf_op jit(solution)/shard_map/broadcast_in_dim | solution.py:500
  2.3 1.2 %broadcast_in_dim.8 = f32[8,32,4,2,64]{4,3,2,1,0:T(2,128)S(1)} broadcast(f32[8,32,4,2]{3,2,1,0:T(4,128)S(1)} %copy.12), dimensions={0,1,2,3} | broadcast | bytes 532480 | tf_op jit(solution)/shard_map/broadcast_in_dim | solution.py:500
  3.6 0.8 reshape.11
  4.4 0.0 copy-start
  4.4 0.0 copy-start.1
  4.4 0.0 copy-start.2
  4.4 0.0 copy-start.3
  4.4 1.0 %pad.4.cexp = f32[8,32,8,128]{3,2,1,0:T(8,128)} pad(f32[8,32,4,128]{3,2,1,0:T(4,128)S(1)} %reshape.11, f32[]{:T(128)} %constant.10.clone.1), padding=0_0x0_0x0_4x0_0 | pad | bytes 1572868 | tf_op jit(solution)/shard_map/jit(_pad)/pad | solution.py:503
  5.5 0.0 copy-done
  5.5 0.0 copy-done.1
  5.5 0.0 copy-done.2
  5.5 0.0 copy-done.3
  5.5 72.1 %shard_map.103 = (f32[16,128,128]{2,1,0:T(8,128)S(1)}, f32[16,128,128]{2,1,0:T(8,128)}, f32[16,128,128]{2,1,0:T(8,128)}) custom-call(f32[16,128,128]{2,1,0:T(8,128)} %src.1, f32[16,128,128]{2,1,0:T(8,128)} %rea.1, f32[16,128,128]{2,1,0:T(8,128)} %con.1, f32[8,32,8,128]{3,2,1,0:T(8,128)} %pad.4.cexp, bf16[256,256]{1,0:T(8,128)(2,1)S(1)} %copy-done, ...), custom_call_target="tpu_custom_call" | custom-call | tf_op jit(solution)/shard_map/pallas_call | solution.py:524
  77.5 0.0 copy-start.5
  77.5 1.0 %copy.16 = f32[16,128,128]{2,1,0:T(8,128)} copy(f32[16,128,128]{2,1,0:T(8,128)S(1)} %get-tuple-element.6) | data formatting | bytes 2097152
  78.5 0.6 copy-done.5
  79.1 0.0 copy-start.4
  79.1 1.0 %copy.17 = f32[16,128,128]{2,1,0:T(8,128)} copy(f32[16,128,128]{2,1,0:T(8,128)S(1)} %copy-done.5) | data formatting | bytes 2097152
  80.1 0.6 copy-done.4
  80.7 1.0 %copy.18 = f32[16,128,128]{2,1,0:T(8,128)} copy(f32[16,128,128]{2,1,0:T(8,128)S(1)} %copy-done.4) | data formatting | bytes 2097152
Async XLA Ops:
  4.4 1.1 %copy-start = (bf16[256,256]{1,0:T(8,128)(2,1)S(1)}, bf16[256,256]{1,0:T(8,128)(2,1)}, u32[]{:S(2)}) copy-start(bf16[256,256]{1,0:T(8,128)(2,1)} %constant.11.clone.tabz) | copy-start | bytes 393220
  4.4 1.1 %copy-start.1 = (f32[128,1]{1,0:T(8,128)S(1)}, f32[128,1]{1,0:T(8,128)}, u32[]{:S(2)}) copy-start(f32[128,1]{1,0:T(8,128)} %constant.13.clone.eigy) | copy-start | bytes 1540
  4.4 1.1 %copy-start.2 = (bf16[128,256]{1,0:T(8,128)(2,1)S(1)}, bf16[128,256]{1,0:T(8,128)(2,1)}, u32[]{:S(2)}) copy-start(bf16[128,256]{1,0:T(8,128)(2,1)} %constant.12.clone.taby) | copy-start | bytes 196612
  4.4 1.1 %copy-start.3 = (f32[1,128]{1,0:T(1,128)S(1)}, f32[1,128]{1,0:T(1,128)}, u32[]{:S(2)}) copy-start(f32[1,128]{1,0:T(1,128)} %constant.14.clone.eigz) | copy-start | bytes 1540
  77.5 1.6 %copy-start.5 = (f32[16,128,128]{2,1,0:T(8,128)S(1)}, f32[16,128,128]{2,1,0:T(8,128)}, u32[]{:S(2)}) copy-start(f32[16,128,128]{2,1,0:T(8,128)} %get-tuple-element.7) | copy-start | bytes 3145732
  79.1 1.6 %copy-start.4 = (f32[16,128,128]{2,1,0:T(8,128)S(1)}, f32[16,128,128]{2,1,0:T(8,128)}, u32[]{:S(2)}) copy-start(f32[16,128,128]{2,1,0:T(8,128)} %get-tuple-element.8) | copy-start | bytes 3145732

commit v2 on v1

--- a/solution.py
+++ b/solution.py
@@ -34,10 +34,10 @@
 
 
 def kernel(
-    nw, nn, src, rea, con, cexp, tabz, taby, eigy, eigz, x_out, r_out, d_out,
-    spec_r, spec_w0, spec_w1, own, total, tail, head, cp, inv, fx, fy, fylo, fz,
+    nw, nn, src, rea, con, cinv, tabz, taby, eigy, eigz, x_out, r_out, d_out,
+    spec, own, total, total0, total1, tail, head, cp, inv, fx, fy, fylo, fz,
     z0, z1, w0, w1, chx, chy, cys, pqs, pqr, yr, hx, hy, hys, ga, gb, gc, gd,
-    nsend, nrecv, gs1, gr1, gs2, gr2,
+    wide_rows, nsend, nrecv, gs1, gr1, gs2, gr2,
 ):
     bx, by, bz = src.shape
     iw, inn = lax.axis_index("wide"), lax.axis_index("narrow")
@@ -198,7 +198,7 @@
         )
         return both[:, :bz] + both[:, bz:]
 
-    step = 4
+    step = bx
 
     def forward(field, out):
         def one(k, carry):
@@ -232,17 +232,16 @@
 
     chunks(eliminate)
 
-    def solve(turn, prepare):
+    def solve(turn, out):
         def ends(rows):
-            prepare(rows)
             value = jnp.zeros((chunk, bz), f32)
             for k in range(W):
-                value = (spec_r[bx - W + k, rows, :] + value) * cp[k, rows, :]
+                value = (spec[bx - W + k, rows, :] + value) * cp[k, rows, :]
                 tail[k, rows, :] = value
             pqs[turn, 1, rows, :] = value
             value = jnp.zeros((chunk, bz), f32)
             for t in reversed(range(W)):
-                value = (spec_r[t, rows, :] + value) * cp[W - 1 - t, rows, :]
+                value = (spec[t, rows, :] + value) * cp[W - 1 - t, rows, :]
                 head[t, rows, :] = value
             pqs[turn, 0, rows, :] = value
 
@@ -255,7 +254,7 @@
         def middle(rows):
             value = pqr[turn, 0, rows, :]
             for t in range(bx):
-                value = (spec_r[t, rows, :] + value) * cp[W + t, rows, :]
+                value = (spec[t, rows, :] + value) * cp[W + t, rows, :]
                 if t < bx - 1:
                     own[t, rows, :] = value
             value = (value + cp[W + bx - 1, rows, :] * pqr[turn, 1, rows, :]) * inv[rows, :]
@@ -275,11 +274,11 @@
             for k in reversed(range(W)):
                 value = tail[k, rows, :] + cp[k, rows, :] * value
                 t = bx - W + k
-                total[t, rows, :] = own[t, rows, :] + on_right * value
+                out[t, rows, :] = own[t, rows, :] + on_right * value
             value = yr[turn, 0, rows, :]
             for t in range(W):
                 value = head[t, rows, :] + cp[W - 1 - t, rows, :] * value
-                total[t, rows, :] = own[t, rows, :] + on_left * value
+                out[t, rows, :] = own[t, rows, :] + on_left * value
 
         chunks(fold)
         each(rims, "leave")
@@ -288,34 +287,44 @@
 
     lanes = lax.broadcasted_iota(jnp.int32, (1, bz), 1)
 
-    def inverse(correction, out):
-        for part in range(2):
-            spread = []
-            for side in range(2):
-                o = part * 4 + side * 2
-                row = jnp.where(lanes < bz // 2, correction[o], correction[o + 1])
-                spread.append(jnp.broadcast_to(row, (half_y, bz)))
-            spread = jnp.concatenate(spread, axis=0)
-
-            def one(k, carry):
-                value = jnp.concatenate(
-                    [along_y(total[k * step + j]) for j in range(step)], axis=0
+    def inverse(correction, out, combine):
+        spread = []
+        for o in range(0, PRIMAL, 2):
+            row = jnp.where(lanes < bz // 2, correction[o], correction[o + 1])
+            spread.append(jnp.broadcast_to(row, (half_y, bz)))
+        spread = [jnp.concatenate(spread[o : o + 2], axis=0) for o in (0, 2)]
+        value = along_z(jnp.concatenate([along_y(combine(x)) for x in range(bx)], axis=0))
+        for x in range(bx):
+            out[x] = value[x * by : (x + 1) * by] + spread[x // half_x]
+
+    scale = 1.0 / (half_x * half_y * (bz // 2))
+
+    def correct(ref):
+        both = jnp.dot(
+            wide_rows[...], ref[...].reshape(nw * nn * 8, bz),
+            precision=lax.Precision.HIGHEST, preferred_element_type=f32,
+        )
+        upper = lax.broadcasted_iota(jnp.int32, (2 * PRIMAL, bz), 1) >= bz // 2
+        second = lax.broadcasted_iota(jnp.int32, (2 * PRIMAL, bz), 0) >= PRIMAL
+        both = jnp.sum(jnp.where(upper == second, both, 0.0), axis=1, keepdims=True)
+        both = (both[:PRIMAL] + both[PRIMAL:]) * scale
+        return [both[o : o + 1] for o in range(PRIMAL)]
+
+    def lay_out():
+        block = 128
+        entry = lax.broadcasted_iota(jnp.int32, (block, block), 0)
+        place_of = lax.broadcasted_iota(jnp.int32, (block, block), 1)
+        device, row = place_of // 8, place_of % 8
+        for side in range(2):
+            chosen = jnp.where((row < 4) & (entry == device * 8 + 2 * row + side), 1.0, 0.0)
+            for k in range(nw * nn * 8 // block):
+                columns = slice(k * block, (k + 1) * block)
+                wide_rows[side * PRIMAL : (side + 1) * PRIMAL, columns] = jnp.dot(
+                    cinv[0, 0, :, columns], chosen.astype(f32),
+                    precision=lax.Precision.HIGHEST, preferred_element_type=f32,
                 )
-                value = along_z(value)
-                for j in range(step):
-                    out[k * step + j] = value[j * by : (j + 1) * by] + spread
-                return carry
-
-            lax.fori_loop(part * (half_x // step), (part + 1) * (half_x // step), one, 0)
-
-    scale = 1.0 / (half_x * half_y * (bz // 2))
-
-    def everything(value):
-        return jnp.sum(jnp.sum(value, axis=0, keepdims=True), axis=1, keepdims=True)
-
-    def correct(ref):
-        message = ref[...].reshape(nw * nn, 8, bz)
-        return [everything(jnp.sum(message * cexp[o], axis=0)) * scale for o in range(PRIMAL)]
+
+    lay_out()
 
     def dots(ref):
         whole = jnp.sum(ref[...].reshape(nw * nn, 8, bz), axis=0)
@@ -360,8 +369,6 @@
             hys.at[turn, 0], hys.at[turn, 1], hy.at[turn], slot + 2, "narrow"
         )
         each(layers, "start")
-        if turn == 0:
-            weights()
         each(layers, "arrive")
 
         def point(x, below, above):
@@ -393,7 +400,8 @@
             else:
                 low, high = half_x, bx - 1
             carry = lax.fori_loop(
-                low, high, lambda x, c: gather_up(x, field[x - 1], field[x + 1], c), carry
+                low, high, lambda x, c: gather_up(x, field[x - 1], field[x + 1], c), carry,
+                    unroll=True,
             )
             if part == 1:
                 carry = gather_up(bx - 1, field[bx - 2], hx[turn, 1], carry)
@@ -402,37 +410,35 @@
         each(layers, "leave")
         return sums + products + [zero8]
 
-    def local(turn, prepare, between=None):
-        stages = solve(turn, prepare)
+    def local(turn, out, gather, between):
+        stages = solve(turn, out)
         next(stages)
-        if between is not None:
-            between()
+        gather.second()
         next(stages)
+        between()
         next(stages)
-
-    forward(src, spec_r)
-    gather_a.second()
-    local(0, lambda rows: None)
-    gather_a.finish()
+        gather.finish()
+
+    forward(src, spec)
+    local(0, total, gather_a, weights)
     coarse = correct(ga)
-    inverse(coarse, z0)
+    inverse(coarse, z0, lambda x: total[x])
     post(gb, apply(0, z0, w0, lambda x, v, a: (src[x] * v, v * a, zero8)))
     gather_b.first()
 
-    forward(w0, spec_w0)
-    gather_b.second()
-    gather_b.finish()
+    forward(w0, spec)
+    local(1, total0, gather_b, lambda: None)
     gamma0, delta0, _ = dots(gb)
     alpha0 = gamma0 / delta0
-
-    def first_step(rows):
-        for t in range(bx):
-            spec_r[t, rows, :] = spec_r[t, rows, :] - alpha0 * spec_w0[t, rows, :]
-
-    local(1, first_step)
     coarse_b = correct(gb)
     coarse = [a - alpha0 * b for a, b in zip(coarse, coarse_b)]
-    inverse(coarse, z1)
+
+    def first_step(x):
+        value = total[x] - alpha0 * total0[x]
+        total[x] = value
+        return value
+
+    inverse(coarse, z1, first_step)
 
     def inner(x, value, result):
         image = w0[x]
@@ -441,17 +447,11 @@
     post(gc, apply(1, z1, w1, inner))
     gather_c.first()
 
-    forward(w1, spec_w1)
-    gather_c.second()
-    gather_c.finish()
+    forward(w1, spec)
+    local(2, total1, gather_c, lambda: None)
     gamma1, own1, cross1 = dots(gc)
     beta1 = gamma1 / gamma0
     alpha1 = gamma1 / (own1 + 2.0 * beta1 * cross1 + beta1 * beta1 * delta0)
-
-    def second_step(rows):
-        for t in range(bx):
-            image = spec_w1[t, rows, :] + beta1 * spec_w0[t, rows, :]
-            spec_r[t, rows, :] = spec_r[t, rows, :] - alpha1 * image
 
     def results():
         def one(x, carry):
@@ -462,24 +462,33 @@
             z1[x] = direction
             return carry
 
-        lax.fori_loop(0, bx, one, 0)
-
-    local(2, second_step, results)
+        lax.fori_loop(0, bx, one, 0, unroll=4)
+
     coarse_c = correct(gc)
     coarse = [a - alpha1 * (c + beta1 * b) for a, b, c in zip(coarse, coarse_b, coarse_c)]
-    inverse(coarse, w1)
-    product = lax.fori_loop(0, bx, lambda x, c: c + fold8(r_out[x] * w1[x]), zero8)
+    inverse(
+        coarse, d_out,
+        lambda x: total[x] - alpha1 * (total1[x] + beta1 * total0[x]),
+    )
+
+    def last_product(x, carry):
+        image = w0[x]
+        remaining = (src[x] - alpha0 * image) - alpha1 * (w1[x] + beta1 * image)
+        return carry + fold8(remaining * d_out[x])
+
+    product = lax.fori_loop(0, bx, last_product, zero8, unroll=4)
     post(gd, [zero8] * 4 + [product] + [zero8] * 3)
     gather_d.first()
     gather_d.second()
+    results()
     gather_d.finish()
     beta2 = dots(gd)[0] / gamma1
 
     def last(x, carry):
-        d_out[x] = w1[x] + beta2 * z1[x]
+        d_out[x] = d_out[x] + beta2 * z1[x]
         return carry
 
-    lax.fori_loop(0, bx, last, 0)
+    lax.fori_loop(0, bx, last, 0, unroll=4)
 
 
 def body(nw, nn, source, reaction, conductance, coarse_inverse):
@@ -496,11 +505,6 @@
     tab_y = parts(table_y)
     tab_z = parts(table_z)
     tab_z = np.concatenate([tab_z, tab_z], axis=0)
-    rows = coarse_inverse.reshape(PRIMAL, nw * nn, 4, 2, 1)
-    rows = jnp.broadcast_to(rows, (PRIMAL, nw * nn, 4, 2, bz // 2)).reshape(
-        PRIMAL, nw * nn, 4, bz
-    )
-    rows = jnp.pad(rows, ((0, 0), (0, 0), (0, 4), (0, 0)))
     block = (bx, by, bz)
     layer = (by, bz)
 
@@ -516,6 +520,7 @@
         vm(3, 2, *layer), vm(3, 2, *layer), vm(3, 2, *layer),
         vm(2, 2, *layer), vm(2, 2, bx, bz), vm(2, 2, bx, bz),
         vm(nw, nn, 8, bz), vm(nw, nn, 8, bz), vm(nw, nn, 8, bz), vm(nw, nn, 8, bz),
+        vm(2 * PRIMAL, nw * nn * 8),
         pltpu.SemaphoreType.DMA((24,)), pltpu.SemaphoreType.DMA((24,)),
         pltpu.SemaphoreType.DMA((4, nn)), pltpu.SemaphoreType.DMA((4, nn)),
         pltpu.SemaphoreType.DMA((4, nw)), pltpu.SemaphoreType.DMA((4, nw)),
@@ -528,10 +533,10 @@
         out_specs=[spec] * 3,
         scratch_shapes=scratch,
         compiler_params=pltpu.CompilerParams(
-            collective_id=0, has_side_effects=True, vmem_limit_bytes=52 * 1024 * 1024
+            collective_id=0, has_side_effects=True, vmem_limit_bytes=32 * 1024 * 1024
         ),
     )(
-        source, reaction, conductance, rows,
+        source, reaction, conductance, coarse_inverse,
         jnp.asarray(tab_z), jnp.asarray(tab_y),
         jnp.asarray(eigen_y.reshape(-1, 1), f32), jnp.asarray(eigen_z.reshape(1, -1), f32),
     )

time: 82 us -> 63.5 us (0.77)
  Pallas kernels: 72.1 us -> 52 us
  local copies, waits for them, and re-layouts: 8.94 us -> 10.5 us
    pallas_call x1, Pallas kernels: 72.1 us -> 52 us  [body(): pl.pallas_call(functools.partial(kernel, nw, nn), out_shape=[jax.ShapeDty...]
    unnamed x16 -> x19, local copies, waits for them, and re-layouts: 5.01 us -> 10.5 us
    broadcast_in_dim x2 -> x0, local copies, waits for them, and re-layouts: 2.13 us -> none  [body(): jnp.broadcast_to(rows, (PRIMAL, nw * nn, 4, 2, bz // 2))]
    pad x1 -> x0, local copies, waits for them, and re-layouts: 1.05 us -> none  [body(): rows = jnp.pad(rows, ((0, 0), (0, 0), (0, 4), (0, 0)))]
where the time goes in v2:
time: 63.5 us; the launch traced here: 63.2 us
  Pallas kernels  52 us (82%)
  local copies, waits for them, and re-layouts  10.5 us (17%)
  between operations  0.66 us (1%)
    pallas_call x1, Pallas kernels, body(): pl.pallas_call(functools.partial(kernel, nw, nn), out_shape=[jax.ShapeDty...  52 us
    unnamed x19, local copies, waits for them, and re-layouts  10.5 us

profile of v2, /device:TPU:0, one launch (start us, length us, event | category | flops | bytes accessed | tf_op | source)
XLA Modules:
  0.0 63.2 jit_solution(7972345908800566899)
XLA Ops:
  0.6 0.0 copy-start.7
  0.6 0.6 %copy-done.7 = f32[1,128]{1,0:T(1,128)S(1)} copy-done((f32[1,128]{1,0:T(1,128)S(1)}, f32[1,128]{1,0:T(1,128)}, u32[]{:S(2)}) %copy-start.7) | copy-done | bytes 536
  1.3 0.0 copy-start
  1.3 1.2 %copy-done = f32[16,128,128]{2,1,0:T(8,128)S(1)} copy-done((f32[16,128,128]{2,1,0:T(8,128)S(1)}, f32[16,128,128]{2,1,0:T(8,128)}, u32[]{:S(2)}) %copy-start) | copy-done | bytes 1048600
  2.5 0.0 copy-start.1
  2.5 1.2 %copy-done.1 = f32[16,128,128]{2,1,0:T(8,128)S(1)} copy-done((f32[16,128,128]{2,1,0:T(8,128)S(1)}, f32[16,128,128]{2,1,0:T(8,128)}, u32[]{:S(2)}) %copy-start.1) | copy-done | bytes 1048600
  3.7 0.0 copy-start.2
  3.7 1.2 %copy-done.2 = f32[16,128,128]{2,1,0:T(8,128)S(1)} copy-done((f32[16,128,128]{2,1,0:T(8,128)S(1)}, f32[16,128,128]{2,1,0:T(8,128)}, u32[]{:S(2)}) %copy-start.2) | copy-done | bytes 1048600
  5.0 0.0 copy-start.3
  5.0 0.9 %copy-done.3 = bf16[256,256]{1,0:T(8,128)(2,1)S(1)} copy-done((bf16[256,256]{1,0:T(8,128)(2,1)S(1)}, bf16[256,256]{1,0:T(8,128)(2,1)}, u32[]{:S(2)}) %copy-start.3) | copy-done | bytes 131096
  5.9 0.0 copy-start.4
  5.9 0.8 %copy-done.4 = f32[128,1]{1,0:T(8,128)S(1)} copy-done((f32[128,1]{1,0:T(8,128)S(1)}, f32[128,1]{1,0:T(8,128)}, u32[]{:S(2)}) %copy-start.4) | copy-done | bytes 536
  6.7 0.0 copy-start.5
  6.7 0.8 %copy-done.5 = bf16[128,256]{1,0:T(8,128)(2,1)S(1)} copy-done((bf16[128,256]{1,0:T(8,128)(2,1)S(1)}, bf16[128,256]{1,0:T(8,128)(2,1)}, u32[]{:S(2)}) %copy-start.5) | copy-done | bytes 65560
  7.6 0.0 copy-start.6
  7.6 0.7 %copy-done.6 = f32[1,1,8,256]{3,2,1,0:T(8,128)S(1)} copy-done((f32[1,1,8,256]{3,2,1,0:T(8,128)S(1)}, f32[1,1,8,256]{3,2,1,0:T(8,128)}, u32[]{:S(2)}) %copy-start.6) | copy-done | bytes 8216
  8.2 52.0 %shard_map.103 = (f32[16,128,128]{2,1,0:T(8,128)S(1)}, f32[16,128,128]{2,1,0:T(8,128)S(1)}, f32[16,128,128]{2,1,0:T(8,128)S(1)}) custom-call(f32[16,128,128]{2,1,0:T(8,128)S(1)} %copy-done, f32[16,128,128]{2,1,0:T(8,128)S(1)} %copy-done.1, f32[16,128,128]{2,1,0:T(8,128)S(1)} %copy-done.2, f32[1,1,8,256]{3,2,1,0:T(8,128)S(1)} %copy-done.6, ...), custom_call_target="tpu_custom_call" | custom-call | tf_op jit(solution)/shard_map/pallas_call | solution.py:529
  60.2 1.0 %copy.14 = f32[16,128,128]{2,1,0:T(8,128)} copy(f32[16,128,128]{2,1,0:T(8,128)S(1)} %get-tuple-element.6) | data formatting | bytes 2097152
  61.2 1.0 %copy.15 = f32[16,128,128]{2,1,0:T(8,128)} copy(f32[16,128,128]{2,1,0:T(8,128)S(1)} %get-tuple-element.7) | data formatting | bytes 2097152
  62.2 1.0 %copy.16 = f32[16,128,128]{2,1,0:T(8,128)} copy(f32[16,128,128]{2,1,0:T(8,128)S(1)} %get-tuple-element.8) | data formatting | bytes 2097152
Async XLA Ops:
  0.6 0.7 %copy-start.7 = (f32[1,128]{1,0:T(1,128)S(1)}, f32[1,128]{1,0:T(1,128)}, u32[]{:S(2)}) copy-start(f32[1,128]{1,0:T(1,128)} %constant.11.clone.eigz) | copy-start | bytes 1540
  1.3 1.2 %copy-start = (f32[16,128,128]{2,1,0:T(8,128)S(1)}, f32[16,128,128]{2,1,0:T(8,128)}, u32[]{:S(2)}) copy-start(f32[16,128,128]{2,1,0:T(8,128)} %src.1) | copy-start | bytes 3145732
  2.5 1.2 %copy-start.1 = (f32[16,128,128]{2,1,0:T(8,128)S(1)}, f32[16,128,128]{2,1,0:T(8,128)}, u32[]{:S(2)}) copy-start(f32[16,128,128]{2,1,0:T(8,128)} %rea.1) | copy-start | bytes 3145732
  3.7 1.2 %copy-start.2 = (f32[16,128,128]{2,1,0:T(8,128)S(1)}, f32[16,128,128]{2,1,0:T(8,128)}, u32[]{:S(2)}) copy-start(f32[16,128,128]{2,1,0:T(8,128)} %con.1) | copy-start | bytes 3145732
  5.0 0.9 %copy-start.3 = (bf16[256,256]{1,0:T(8,128)(2,1)S(1)}, bf16[256,256]{1,0:T(8,128)(2,1)}, u32[]{:S(2)}) copy-start(bf16[256,256]{1,0:T(8,128)(2,1)} %constant.8.clone.tabz) | copy-start | bytes 393220
  5.9 0.8 %copy-start.4 = (f32[128,1]{1,0:T(8,128)S(1)}, f32[128,1]{1,0:T(8,128)}, u32[]{:S(2)}) copy-start(f32[128,1]{1,0:T(8,128)} %constant.10.clone.eigy) | copy-start | bytes 1540
  6.7 0.8 %copy-start.5 = (bf16[128,256]{1,0:T(8,128)(2,1)S(1)}, bf16[128,256]{1,0:T(8,128)(2,1)}, u32[]{:S(2)}) copy-start(bf16[128,256]{1,0:T(8,128)(2,1)} %constant.9.clone.taby) | copy-start | bytes 196612
  7.6 0.7 %copy-start.6 = (f32[1,1,8,256]{3,2,1,0:T(8,128)S(1)}, f32[1,1,8,256]{3,2,1,0:T(8,128)}, u32[]{:S(2)}) copy-start(f32[1,1,8,256]{3,2,1,0:T(8,128)} %cinv.1) | copy-start | bytes 24580

commit v3 on v2

--- a/solution.py
+++ b/solution.py
@@ -35,7 +35,7 @@
 
 def kernel(
     nw, nn, src, rea, con, cinv, tabz, taby, eigy, eigz, x_out, r_out, d_out,
-    spec, own, total, total0, total1, tail, head, cp, inv, fx, fy, fylo, fz,
+    spec, spec0, spec1, own, total, total0, total1, tail, head, cp, inv, fx, fy, fylo, fyhi, fz,
     z0, z1, w0, w1, chx, chy, cys, pqs, pqr, yr, hx, hy, hys, ga, gb, gc, gd,
     wide_rows, nsend, nrecv, gs1, gr1, gs2, gr2,
 ):
@@ -58,7 +58,6 @@
 
     greet("wide")
     greet("narrow")
-    pl.semaphore_wait(barrier, nw + nn - 2)
 
     class Shift:
         def __init__(self, source, target, slot, axis, step):
@@ -155,8 +154,6 @@
     cys[1] = con[:, by - 1, :]
     cond_x = pair(con.at[0], con.at[bx - 1], chx, 0, "wide")
     cond_y = pair(cys.at[0], cys.at[1], chy, 2, "narrow")
-    each(cond_x + cond_y, "start")
-
     def fold8(value):
         return value.reshape(value.shape[0] // 8, 8, bz).sum(axis=0)
 
@@ -181,7 +178,6 @@
         Gather(ref, slot) for slot, ref in enumerate((ga, gb, gc, gd))
     )
     post(ga, means_of(src) + [zero8] * 4)
-    gather_a.first()
 
     def along_z(value):
         high, low = split(value)
@@ -232,7 +228,7 @@
 
     chunks(eliminate)
 
-    def solve(turn, out):
+    def solve(turn, spec, out):
         def ends(rows):
             value = jnp.zeros((chunk, bz), f32)
             for k in range(W):
@@ -332,12 +328,6 @@
 
     index_y = lax.broadcasted_iota(jnp.int32, (by, bz), 0)
 
-    def shifted_down(value, low):
-        return jnp.where(index_y == 0, low, pltpu.roll(value, 1, 0))
-
-    def shifted_up(value, high):
-        return jnp.where(index_y == by - 1, high, pltpu.roll(value, by - 1, 0))
-
     def weights():
         each(cond_x + cond_y, "arrive")
         index_z = lax.broadcasted_iota(jnp.int32, (by, bz), 1)
@@ -346,7 +336,9 @@
 
         def one(x, carry):
             value = con[x]
-            fy[x] = harmonic(value, shifted_up(value, chy[1, pl.ds(x, 1), :]))
+            fy[x] = jnp.where(
+                index_y == by - 1, 0.0, harmonic(value, pltpu.roll(value, by - 1, 0))
+            )
             fz[x] = jnp.where(
                 index_z == bz - 1, 0.0, harmonic(value, pltpu.roll(value, bz - 1, 1))
             )
@@ -359,6 +351,7 @@
         lax.fori_loop(0, bx, one, 0)
         lax.fori_loop(1, bx, between, 0)
         fylo[...] = harmonic(cys[0], chy[0])
+        fyhi[...] = harmonic(cys[1], chy[1])
         each(cond_x + cond_y, "leave")
 
     def apply(turn, field, out, inner):
@@ -369,21 +362,17 @@
             hys.at[turn, 0], hys.at[turn, 1], hy.at[turn], slot + 2, "narrow"
         )
         each(layers, "start")
-        each(layers, "arrive")
 
         def point(x, below, above):
             value = field[x]
             result = rea[x] * value
             result = result + fx[x + 1] * (value - above) + fx[x] * (value - below)
-            flux = fy[x] * (value - shifted_up(value, hy[turn, 1, pl.ds(x, 1), :]))
-            low = fylo[pl.ds(x, 1), :] * (hy[turn, 0, pl.ds(x, 1), :] - value[0:1])
-            result = result + flux - shifted_down(flux, low)
+            flux = fy[x] * (value - pltpu.roll(value, by - 1, 0))
+            result = result + flux - pltpu.roll(flux, 1, 0)
             flux = fz[x] * (value - pltpu.roll(value, bz - 1, 1))
             result = result + flux - pltpu.roll(flux, 1, 1)
             out[x] = result
             return value, result
-
-        sums, products = [], [zero8] * 3
 
         def gather_up(x, below, above, carry):
             value, result = point(x, below, above)
@@ -392,26 +381,37 @@
                 carry[0] + fold8(result[:half_y]), carry[1] + fold8(result[half_y:]),
             ) + tuple(c + fold8(e) for c, e in zip(carry[2:], extra))
 
+        parts = []
+        products = (zero8,) * 3
+        for low, high in ((1, half_x), (half_x, bx - 1)):
+            carry = lax.fori_loop(
+                low, high, lambda x, c: gather_up(x, field[x - 1], field[x + 1], c),
+                (zero8, zero8) + products, unroll=True,
+            )
+            parts.append(carry[:2])
+            products = carry[2:]
+        each(layers, "arrive")
+        carry = gather_up(0, hx[turn, 0], field[1], parts[0] + products)
+        parts[0] = carry[:2]
+        carry = gather_up(bx - 1, field[bx - 2], hx[turn, 1], parts[1] + carry[2:])
+        parts[1] = carry[:2]
+        products = list(carry[2:])
+        low = fylo[...] * (hys[turn, 0] - hy[turn, 0])
+        high = fyhi[...] * (hys[turn, 1] - hy[turn, 1])
+        out[:, 0, :] = out[:, 0, :] + low
+        out[:, by - 1, :] = out[:, by - 1, :] + high
+        products[1] = products[1] + fold8(hys[turn, 0] * low + hys[turn, 1] * high)
+        sums = []
         for part in range(2):
-            carry = (zero8, zero8) + tuple(products)
-            if part == 0:
-                carry = gather_up(0, hx[turn, 0], field[1], carry)
-                low, high = 1, half_x
-            else:
-                low, high = half_x, bx - 1
-            carry = lax.fori_loop(
-                low, high, lambda x, c: gather_up(x, field[x - 1], field[x + 1], c), carry,
-                    unroll=True,
-            )
-            if part == 1:
-                carry = gather_up(bx - 1, field[bx - 2], hx[turn, 1], carry)
-            sums += [carry[0], carry[1]]
-            products = list(carry[2:])
+            planes = slice(part * half_x, (part + 1) * half_x)
+            sums += [
+                parts[part][0] + fold8(low[planes]), parts[part][1] + fold8(high[planes]),
+            ]
         each(layers, "leave")
         return sums + products + [zero8]
 
-    def local(turn, out, gather, between):
-        stages = solve(turn, out)
+    def local(turn, field, out, gather, between):
+        stages = solve(turn, field, out)
         next(stages)
         gather.second()
         next(stages)
@@ -420,14 +420,17 @@
         gather.finish()
 
     forward(src, spec)
-    local(0, total, gather_a, weights)
+    pl.semaphore_wait(barrier, nw + nn - 2)
+    each(cond_x + cond_y, "start")
+    gather_a.first()
+    local(0, spec, total, gather_a, weights)
     coarse = correct(ga)
     inverse(coarse, z0, lambda x: total[x])
     post(gb, apply(0, z0, w0, lambda x, v, a: (src[x] * v, v * a, zero8)))
     gather_b.first()
 
-    forward(w0, spec)
-    local(1, total0, gather_b, lambda: None)
+    forward(w0, spec0)
+    local(1, spec0, total0, gather_b, lambda: None)
     gamma0, delta0, _ = dots(gb)
     alpha0 = gamma0 / delta0
     coarse_b = correct(gb)
@@ -447,8 +450,8 @@
     post(gc, apply(1, z1, w1, inner))
     gather_c.first()
 
-    forward(w1, spec)
-    local(2, total1, gather_c, lambda: None)
+    forward(w1, spec1)
+    local(2, spec1, total1, gather_c, lambda: None)
     gamma1, own1, cross1 = dots(gc)
     beta1 = gamma1 / gamma0
     alpha1 = gamma1 / (own1 + 2.0 * beta1 * cross1 + beta1 * beta1 * delta0)
@@ -466,23 +469,31 @@
 
     coarse_c = correct(gc)
     coarse = [a - alpha1 * (c + beta1 * b) for a, b, c in zip(coarse, coarse_b, coarse_c)]
-    inverse(
-        coarse, d_out,
-        lambda x: total[x] - alpha1 * (total1[x] + beta1 * total0[x]),
+
+    def last_product(x, carry):
+        value = total[x] - alpha1 * (total1[x] + beta1 * total0[x])
+        total[x] = value
+        image = spec0[x]
+        remaining = (spec[x] - alpha0 * image) - alpha1 * (spec1[x] + beta1 * image)
+        return carry + fold8(remaining * value)
+
+    product = lax.fori_loop(0, bx, last_product, zero8, unroll=4)
+    image_sums = gb[iw, inn]
+    residual_sums = (ga[iw, inn] - alpha0 * image_sums) - alpha1 * (
+        gc[iw, inn] + beta1 * image_sums
     )
-
-    def last_product(x, carry):
-        image = w0[x]
-        remaining = (src[x] - alpha0 * image) - alpha1 * (w1[x] + beta1 * image)
-        return carry + fold8(remaining * d_out[x])
-
-    product = lax.fori_loop(0, bx, last_product, zero8, unroll=4)
-    post(gd, [zero8] * 4 + [product] + [zero8] * 3)
+    coarse_product = jnp.zeros((1, bz), f32)
+    for o in range(0, PRIMAL, 2):
+        row = jnp.where(lanes < bz // 2, coarse[o], coarse[o + 1])
+        coarse_product = coarse_product + residual_sums[o // 2 : o // 2 + 1] * row
+    post(gd, [zero8] * 4 + [product, coarse_product] + [zero8] * 2)
     gather_d.first()
+    results()
     gather_d.second()
-    results()
+    inverse(coarse, d_out, lambda x: total[x])
     gather_d.finish()
-    beta2 = dots(gd)[0] / gamma1
+    parts = dots(gd)
+    beta2 = (parts[0] + parts[1]) / gamma1
 
     def last(x, carry):
         d_out[x] = d_out[x] + beta2 * z1[x]
@@ -512,9 +523,9 @@
         return pltpu.VMEM(shape, f32)
 
     scratch = [
-        vm(*block), vm(*block), vm(*block), vm(*block), vm(*block),
+        vm(*block), vm(*block), vm(*block), vm(*block), vm(*block), vm(*block), vm(*block),
         vm(W, *layer), vm(W, *layer), vm(W + bx, *layer), vm(*layer),
-        vm(bx + 1, *layer), vm(*block), vm(bx, bz), vm(*block),
+        vm(bx + 1, *layer), vm(*block), vm(bx, bz), vm(bx, bz), vm(*block),
         vm(*block), vm(*block), vm(*block), vm(*block),
         vm(2, *layer), vm(2, bx, bz), vm(2, bx, bz),
         vm(3, 2, *layer), vm(3, 2, *layer), vm(3, 2, *layer),

time: 63.5 us -> 59.8 us (0.942)
  Pallas kernels: 52 us -> 48.2 us
    pallas_call x1, Pallas kernels: 52 us -> 48.2 us  [body(): pl.pallas_call(functools.partial(kernel, nw, nn), out_shape=[jax.ShapeDty...]
where the time goes in v3:
time: 59.8 us; the launch traced here: 59.4 us
  Pallas kernels  48.2 us (81%)
  local copies, waits for them, and re-layouts  10.5 us (18%)
  between operations  0.66 us (1%)
    pallas_call x1, Pallas kernels, body(): pl.pallas_call(functools.partial(kernel, nw, nn), out_shape=[jax.ShapeDty...  48.2 us
    unnamed x19, local copies, waits for them, and re-layouts  10.5 us

profile of v3, /device:TPU:0, one launch (start us, length us, event | category | flops | bytes accessed | tf_op | source)
XLA Modules:
  0.0 59.4 jit_solution(5425048960417134693)
XLA Ops:
  0.6 0.0 copy-start.7
  0.6 0.6 %copy-done.7 = f32[1,128]{1,0:T(1,128)S(1)} copy-done((f32[1,128]{1,0:T(1,128)S(1)}, f32[1,128]{1,0:T(1,128)}, u32[]{:S(2)}) %copy-start.7) | copy-done | bytes 536
  1.3 0.0 copy-start
  1.3 1.2 %copy-done = f32[16,128,128]{2,1,0:T(8,128)S(1)} copy-done((f32[16,128,128]{2,1,0:T(8,128)S(1)}, f32[16,128,128]{2,1,0:T(8,128)}, u32[]{:S(2)}) %copy-start) | copy-done | bytes 1048600
  2.5 0.0 copy-start.1
  2.5 1.2 %copy-done.1 = f32[16,128,128]{2,1,0:T(8,128)S(1)} copy-done((f32[16,128,128]{2,1,0:T(8,128)S(1)}, f32[16,128,128]{2,1,0:T(8,128)}, u32[]{:S(2)}) %copy-start.1) | copy-done | bytes 1048600
  3.7 0.0 copy-start.2
  3.7 1.2 %copy-done.2 = f32[16,128,128]{2,1,0:T(8,128)S(1)} copy-done((f32[16,128,128]{2,1,0:T(8,128)S(1)}, f32[16,128,128]{2,1,0:T(8,128)}, u32[]{:S(2)}) %copy-start.2) | copy-done | bytes 1048600
  5.0 0.0 copy-start.3
  5.0 0.9 %copy-done.3 = bf16[256,256]{1,0:T(8,128)(2,1)S(1)} copy-done((bf16[256,256]{1,0:T(8,128)(2,1)S(1)}, bf16[256,256]{1,0:T(8,128)(2,1)}, u32[]{:S(2)}) %copy-start.3) | copy-done | bytes 131096
  5.9 0.0 copy-start.4
  5.9 0.8 %copy-done.4 = f32[128,1]{1,0:T(8,128)S(1)} copy-done((f32[128,1]{1,0:T(8,128)S(1)}, f32[128,1]{1,0:T(8,128)}, u32[]{:S(2)}) %copy-start.4) | copy-done | bytes 536
  6.7 0.0 copy-start.5
  6.7 0.8 %copy-done.5 = bf16[128,256]{1,0:T(8,128)(2,1)S(1)} copy-done((bf16[128,256]{1,0:T(8,128)(2,1)S(1)}, bf16[128,256]{1,0:T(8,128)(2,1)}, u32[]{:S(2)}) %copy-start.5) | copy-done | bytes 65560
  7.6 0.0 copy-start.6
  7.6 0.7 %copy-done.6 = f32[1,1,8,256]{3,2,1,0:T(8,128)S(1)} copy-done((f32[1,1,8,256]{3,2,1,0:T(8,128)S(1)}, f32[1,1,8,256]{3,2,1,0:T(8,128)}, u32[]{:S(2)}) %copy-start.6) | copy-done | bytes 8216
  8.2 48.2 %shard_map.103 = (f32[16,128,128]{2,1,0:T(8,128)S(1)}, f32[16,128,128]{2,1,0:T(8,128)S(1)}, f32[16,128,128]{2,1,0:T(8,128)S(1)}) custom-call(f32[16,128,128]{2,1,0:T(8,128)S(1)} %copy-done, f32[16,128,128]{2,1,0:T(8,128)S(1)} %copy-done.1, f32[16,128,128]{2,1,0:T(8,128)S(1)} %copy-done.2, f32[1,1,8,256]{3,2,1,0:T(8,128)S(1)} %copy-done.6, ...), custom_call_target="tpu_custom_call" | custom-call | tf_op jit(solution)/shard_map/pallas_call | solution.py:540
  56.5 1.0 %copy.14 = f32[16,128,128]{2,1,0:T(8,128)} copy(f32[16,128,128]{2,1,0:T(8,128)S(1)} %get-tuple-element.6) | data formatting | bytes 2097152
  57.4 1.0 %copy.15 = f32[16,128,128]{2,1,0:T(8,128)} copy(f32[16,128,128]{2,1,0:T(8,128)S(1)} %get-tuple-element.7) | data formatting | bytes 2097152
  58.4 1.0 %copy.16 = f32[16,128,128]{2,1,0:T(8,128)} copy(f32[16,128,128]{2,1,0:T(8,128)S(1)} %get-tuple-element.8) | data formatting | bytes 2097152
Async XLA Ops:
  0.6 0.7 %copy-start.7 = (f32[1,128]{1,0:T(1,128)S(1)}, f32[1,128]{1,0:T(1,128)}, u32[]{:S(2)}) copy-start(f32[1,128]{1,0:T(1,128)} %constant.11.clone.eigz) | copy-start | bytes 1540
  1.3 1.2 %copy-start = (f32[16,128,128]{2,1,0:T(8,128)S(1)}, f32[16,128,128]{2,1,0:T(8,128)}, u32[]{:S(2)}) copy-start(f32[16,128,128]{2,1,0:T(8,128)} %src.1) | copy-start | bytes 3145732
  2.5 1.2 %copy-start.1 = (f32[16,128,128]{2,1,0:T(8,128)S(1)}, f32[16,128,128]{2,1,0:T(8,128)}, u32[]{:S(2)}) copy-start(f32[16,128,128]{2,1,0:T(8,128)} %rea.1) | copy-start | bytes 3145732
  3.7 1.2 %copy-start.2 = (f32[16,128,128]{2,1,0:T(8,128)S(1)}, f32[16,128,128]{2,1,0:T(8,128)}, u32[]{:S(2)}) copy-start(f32[16,128,128]{2,1,0:T(8,128)} %con.1) | copy-start | bytes 3145732
  5.0 0.9 %copy-start.3 = (bf16[256,256]{1,0:T(8,128)(2,1)S(1)}, bf16[256,256]{1,0:T(8,128)(2,1)}, u32[]{:S(2)}) copy-start(bf16[256,256]{1,0:T(8,128)(2,1)} %constant.8.clone.tabz) | copy-start | bytes 393220
  5.9 0.8 %copy-start.4 = (f32[128,1]{1,0:T(8,128)S(1)}, f32[128,1]{1,0:T(8,128)}, u32[]{:S(2)}) copy-start(f32[128,1]{1,0:T(8,128)} %constant.10.clone.eigy) | copy-start | bytes 1540
  6.7 0.8 %copy-start.5 = (bf16[128,256]{1,0:T(8,128)(2,1)S(1)}, bf16[128,256]{1,0:T(8,128)(2,1)}, u32[]{:S(2)}) copy-start(bf16[128,256]{1,0:T(8,128)(2,1)} %constant.9.clone.taby) | copy-start | bytes 196612
  7.6 0.7 %copy-start.6 = (f32[1,1,8,256]{3,2,1,0:T(8,128)S(1)}, f32[1,1,8,256]{3,2,1,0:T(8,128)}, u32[]{:S(2)}) copy-start(f32[1,1,8,256]{3,2,1,0:T(8,128)} %cinv.1) | copy-start | bytes 24580

commit v4 on v3

--- a/solution.py
+++ b/solution.py
@@ -283,15 +283,27 @@
 
     lanes = lax.broadcasted_iota(jnp.int32, (1, bz), 1)
 
-    def inverse(correction, out, combine):
+    def inverse(correction, out, combine, turn=None):
         spread = []
         for o in range(0, PRIMAL, 2):
             row = jnp.where(lanes < bz // 2, correction[o], correction[o + 1])
             spread.append(jnp.broadcast_to(row, (half_y, bz)))
         spread = [jnp.concatenate(spread[o : o + 2], axis=0) for o in (0, 2)]
-        value = along_z(jnp.concatenate([along_y(combine(x)) for x in range(bx)], axis=0))
-        for x in range(bx):
-            out[x] = value[x * by : (x + 1) * by] + spread[x // half_x]
+
+        def planes(rows):
+            value = along_z(jnp.concatenate([along_y(combine(x)) for x in rows], axis=0))
+            for k, x in enumerate(rows):
+                out[x] = value[k * by : (k + 1) * by] + spread[x // half_x]
+
+        if turn is None:
+            planes(range(bx))
+        else:
+            planes([0, bx - 1])
+            each(outer_planes(turn, out), "start")
+            planes(range(1, bx - 1))
+
+    def outer_planes(turn, field):
+        return pair(field.at[0], field.at[bx - 1], hx.at[turn], 16 + 4 * turn, "wide")
 
     scale = 1.0 / (half_x * half_y * (bz // 2))
 
@@ -358,10 +370,9 @@
         hys[turn, 0] = field[:, 0, :]
         hys[turn, 1] = field[:, by - 1, :]
         slot = 16 + 4 * turn
-        layers = pair(field.at[0], field.at[bx - 1], hx.at[turn], slot, "wide") + pair(
-            hys.at[turn, 0], hys.at[turn, 1], hy.at[turn], slot + 2, "narrow"
-        )
-        each(layers, "start")
+        sides = pair(hys.at[turn, 0], hys.at[turn, 1], hy.at[turn], slot + 2, "narrow")
+        each(sides, "start")
+        layers = outer_planes(turn, field) + sides
 
         def point(x, below, above):
             value = field[x]
@@ -425,7 +436,7 @@
     gather_a.first()
     local(0, spec, total, gather_a, weights)
     coarse = correct(ga)
-    inverse(coarse, z0, lambda x: total[x])
+    inverse(coarse, z0, lambda x: total[x], 0)
     post(gb, apply(0, z0, w0, lambda x, v, a: (src[x] * v, v * a, zero8)))
     gather_b.first()
 
@@ -441,7 +452,7 @@
         total[x] = value
         return value
 
-    inverse(coarse, z1, first_step)
+    inverse(coarse, z1, first_step, 1)
 
     def inner(x, value, result):
         image = w0[x]

time: 59.8 us -> 59.4 us (level)
  no operation moved by 1% of the time
where the time goes in v4:
time: 59.4 us; the launch traced here: 59 us
  Pallas kernels  47.9 us (81%)
  local copies, waits for them, and re-layouts  10.5 us (18%)
  between operations  0.66 us (1%)
    pallas_call x1, Pallas kernels, body(): pl.pallas_call(functools.partial(kernel, nw, nn), out_shape=[jax.ShapeDty...  47.9 us
    unnamed x19, local copies, waits for them, and re-layouts  10.5 us

profile of v4, /device:TPU:0, one launch (start us, length us, event | category | flops | bytes accessed | tf_op | source)
XLA Modules:
  0.0 59.0 jit_solution(3333793662054679514)
XLA Ops:
  0.6 0.0 copy-start.7
  0.6 0.6 %copy-done.7 = f32[1,128]{1,0:T(1,128)S(1)} copy-done((f32[1,128]{1,0:T(1,128)S(1)}, f32[1,128]{1,0:T(1,128)}, u32[]{:S(2)}) %copy-start.7) | copy-done | bytes 536
  1.3 0.0 copy-start
  1.3 1.2 %copy-done = f32[16,128,128]{2,1,0:T(8,128)S(1)} copy-done((f32[16,128,128]{2,1,0:T(8,128)S(1)}, f32[16,128,128]{2,1,0:T(8,128)}, u32[]{:S(2)}) %copy-start) | copy-done | bytes 1048600
  2.5 0.0 copy-start.1
  2.5 1.2 %copy-done.1 = f32[16,128,128]{2,1,0:T(8,128)S(1)} copy-done((f32[16,128,128]{2,1,0:T(8,128)S(1)}, f32[16,128,128]{2,1,0:T(8,128)}, u32[]{:S(2)}) %copy-start.1) | copy-done | bytes 1048600
  3.7 0.0 copy-start.2
  3.7 1.2 %copy-done.2 = f32[16,128,128]{2,1,0:T(8,128)S(1)} copy-done((f32[16,128,128]{2,1,0:T(8,128)S(1)}, f32[16,128,128]{2,1,0:T(8,128)}, u32[]{:S(2)}) %copy-start.2) | copy-done | bytes 1048600
  5.0 0.0 copy-start.3
  5.0 0.9 %copy-done.3 = bf16[256,256]{1,0:T(8,128)(2,1)S(1)} copy-done((bf16[256,256]{1,0:T(8,128)(2,1)S(1)}, bf16[256,256]{1,0:T(8,128)(2,1)}, u32[]{:S(2)}) %copy-start.3) | copy-done | bytes 131096
  5.9 0.0 copy-start.4
  5.9 0.8 %copy-done.4 = f32[128,1]{1,0:T(8,128)S(1)} copy-done((f32[128,1]{1,0:T(8,128)S(1)}, f32[128,1]{1,0:T(8,128)}, u32[]{:S(2)}) %copy-start.4) | copy-done | bytes 536
  6.7 0.0 copy-start.5
  6.7 0.8 %copy-done.5 = bf16[128,256]{1,0:T(8,128)(2,1)S(1)} copy-done((bf16[128,256]{1,0:T(8,128)(2,1)S(1)}, bf16[128,256]{1,0:T(8,128)(2,1)}, u32[]{:S(2)}) %copy-start.5) | copy-done | bytes 65560
  7.6 0.0 copy-start.6
  7.6 0.7 %copy-done.6 = f32[1,1,8,256]{3,2,1,0:T(8,128)S(1)} copy-done((f32[1,1,8,256]{3,2,1,0:T(8,128)S(1)}, f32[1,1,8,256]{3,2,1,0:T(8,128)}, u32[]{:S(2)}) %copy-start.6) | copy-done | bytes 8216
  8.2 47.9 %shard_map.103 = (f32[16,128,128]{2,1,0:T(8,128)S(1)}, f32[16,128,128]{2,1,0:T(8,128)S(1)}, f32[16,128,128]{2,1,0:T(8,128)S(1)}) custom-call(f32[16,128,128]{2,1,0:T(8,128)S(1)} %copy-done, f32[16,128,128]{2,1,0:T(8,128)S(1)} %copy-done.1, f32[16,128,128]{2,1,0:T(8,128)S(1)} %copy-done.2, f32[1,1,8,256]{3,2,1,0:T(8,128)S(1)} %copy-done.6, ...), custom_call_target="tpu_custom_call" | custom-call | tf_op jit(solution)/shard_map/pallas_call | solution.py:551
  56.1 1.0 %copy.14 = f32[16,128,128]{2,1,0:T(8,128)} copy(f32[16,128,128]{2,1,0:T(8,128)S(1)} %get-tuple-element.6) | data formatting | bytes 2097152
  57.1 1.0 %copy.15 = f32[16,128,128]{2,1,0:T(8,128)} copy(f32[16,128,128]{2,1,0:T(8,128)S(1)} %get-tuple-element.7) | data formatting | bytes 2097152
  58.0 1.0 %copy.16 = f32[16,128,128]{2,1,0:T(8,128)} copy(f32[16,128,128]{2,1,0:T(8,128)S(1)} %get-tuple-element.8) | data formatting | bytes 2097152
Async XLA Ops:
  0.6 0.7 %copy-start.7 = (f32[1,128]{1,0:T(1,128)S(1)}, f32[1,128]{1,0:T(1,128)}, u32[]{:S(2)}) copy-start(f32[1,128]{1,0:T(1,128)} %constant.11.clone.eigz) | copy-start | bytes 1540
  1.3 1.2 %copy-start = (f32[16,128,128]{2,1,0:T(8,128)S(1)}, f32[16,128,128]{2,1,0:T(8,128)}, u32[]{:S(2)}) copy-start(f32[16,128,128]{2,1,0:T(8,128)} %src.1) | copy-start | bytes 3145732
  2.5 1.2 %copy-start.1 = (f32[16,128,128]{2,1,0:T(8,128)S(1)}, f32[16,128,128]{2,1,0:T(8,128)}, u32[]{:S(2)}) copy-start(f32[16,128,128]{2,1,0:T(8,128)} %rea.1) | copy-start | bytes 3145732
  3.7 1.2 %copy-start.2 = (f32[16,128,128]{2,1,0:T(8,128)S(1)}, f32[16,128,128]{2,1,0:T(8,128)}, u32[]{:S(2)}) copy-start(f32[16,128,128]{2,1,0:T(8,128)} %con.1) | copy-start | bytes 3145732
  5.0 0.9 %copy-start.3 = (bf16[256,256]{1,0:T(8,128)(2,1)S(1)}, bf16[256,256]{1,0:T(8,128)(2,1)}, u32[]{:S(2)}) copy-start(bf16[256,256]{1,0:T(8,128)(2,1)} %constant.8.clone.tabz) | copy-start | bytes 393220
  5.9 0.8 %copy-start.4 = (f32[128,1]{1,0:T(8,128)S(1)}, f32[128,1]{1,0:T(8,128)}, u32[]{:S(2)}) copy-start(f32[128,1]{1,0:T(8,128)} %constant.10.clone.eigy) | copy-start | bytes 1540
  6.7 0.8 %copy-start.5 = (bf16[128,256]{1,0:T(8,128)(2,1)S(1)}, bf16[128,256]{1,0:T(8,128)(2,1)}, u32[]{:S(2)}) copy-start(bf16[128,256]{1,0:T(8,128)(2,1)} %constant.9.clone.taby) | copy-start | bytes 196612
  7.6 0.7 %copy-start.6 = (f32[1,1,8,256]{3,2,1,0:T(8,128)S(1)}, f32[1,1,8,256]{3,2,1,0:T(8,128)}, u32[]{:S(2)}) copy-start(f32[1,1,8,256]{3,2,1,0:T(8,128)} %cinv.1) | copy-start | bytes 24580
